TPU v7x, 32 devices: a whole 2x2x4 slice. The times are simulated.
32 devices in a mesh: wide: 8 (over y, x, core), narrow: 4 (over z).
Axes of the slice: x: 2, y: 2, z: 4, core: 2. Of those that a mesh axis runs over, the one named last changes fastest.
Arguments:
- start_point: int32 [32768], P(('wide', 'narrow')), may hold values from 0 to 16380
- frac_step: int32 [32768], P(('wide', 'narrow')), may hold values from 0 to 63
- targets: bfloat16 [32768], P(('wide', 'narrow')), may hold values from -6 to 6
- basis_cols: bfloat16 [16384, 2048], P(None, 'narrow'), may hold values from -0.046875 to 0.046875
Outputs:
- q_scaled: float32 [32768, 2048], P(('wide', 'narrow'))
- coefficients: float32 [2048], replicated
All inputs are finite; a program needn't handle non-finite values.
Results may differ from a plain program's by a relative error of at most 0.0037.
Values may be sent and summed in bfloat16 or wider, within the bound.
No kernel may reach another device: no remote copies, remote signals or barrier semaphores. Data moves between devices by JAX's collectives and lax.ppermute only.
A program may use at most 256 MiB of HBM per device.

v0:
```python
import math

import jax
import jax.numpy as jnp
import numpy as np
from jax import lax
from jax.sharding import PartitionSpec as P

upper_rows, upper_cols = np.triu_indices(16)
highest = lax.Precision.HIGHEST


def spline_weights(frac_step):
    position = frac_step.astype(jnp.float32) / 64.0
    first = (1.0 - position) ** 3 / 6.0
    second = (3.0 * position**3 - 6.0 * position**2 + 4.0) / 6.0
    third = (-3.0 * position**3 + 3.0 * position**2 + 3.0 * position + 1.0) / 6.0
    fourth = position**3 / 6.0
    return [first, second, third, fourth]


def project(basis_cols, start_point, frac_step):
    weights = spline_weights(frac_step)
    accumulated = jnp.zeros((start_point.shape[0], basis_cols.shape[1]), jnp.float32)
    for offset in range(4):
        picked = jnp.take(basis_cols, start_point + offset, axis=0).astype(jnp.float32)
        accumulated = accumulated + weights[offset][:, None] * picked
    return accumulated.astype(jnp.bfloat16)


def block_width(order):
    return min(order, 512)


def block_cholesky(gram_total):
    order = gram_total.shape[0]
    width = block_width(order)
    lower = jnp.zeros_like(gram_total)
    for block in range(order // width):
        low = block * width
        high = low + width
        left_part = lower[low:high, :low]
        diag_block = gram_total[low:high, low:high] - jnp.dot(
            left_part, left_part.T, precision=highest
        )
        diag_factor = jnp.linalg.cholesky(diag_block)
        lower = lower.at[low:high, low:high].set(diag_factor)
        if high < order:
            below = gram_total[high:, low:high] - jnp.dot(
                lower[high:, :low], left_part.T, precision=highest
            )
            solved = lax.linalg.triangular_solve(
                diag_factor, below, left_side=False, lower=True, transpose_a=True
            )
            lower = lower.at[high:, low:high].set(solved)
    return lower


def solve_right(chol_lower, panel_float):
    order = chol_lower.shape[0]
    width = block_width(order)
    pieces = []
    for block in range(order // width):
        low = block * width
        high = low + width
        rhs_block = panel_float[:, low:high]
        if low > 0:
            earlier = jnp.concatenate(pieces, axis=1)
            rhs_block = rhs_block - jnp.dot(
                earlier, chol_lower[low:high, :low].T, precision=highest
            )
        pieces.append(
            lax.linalg.triangular_solve(
                chol_lower[low:high, low:high],
                rhs_block,
                left_side=False,
                lower=True,
                transpose_a=True,
            )
        )
    return jnp.concatenate(pieces, axis=1)


def lower_solve(chol_lower, vector):
    order = chol_lower.shape[0]
    width = block_width(order)
    count = order // width
    pieces = {}
    order_list = list(range(count))
    order_list = order_list[::-1]
    for block in order_list:
        low = block * width
        high = low + width
        rhs_block = vector[low:high][:, None]
        if high < order:
            later = jnp.concatenate([pieces[other] for other in range(block + 1, count)], axis=0)
            rhs_block = rhs_block - jnp.dot(chol_lower[high:, low:high].T, later, precision=highest)
        pieces[block] = lax.linalg.triangular_solve(
            chol_lower[low:high, low:high], rhs_block, left_side=True, lower=True, transpose_a=True
        )
    return jnp.concatenate([pieces[other] for other in range(count)], axis=0)[:, 0]


def per_device(start_point, frac_step, targets, basis_cols):
    group_start, group_frac = (
        lax.all_gather(start_point, "narrow", axis=0, tiled=True),
        lax.all_gather(frac_step, "narrow", axis=0, tiled=True),
    )
    columns = project(basis_cols, group_start, group_frac)
    panel = lax.all_to_all(columns, "narrow", split_axis=0, concat_axis=1, tiled=True)
    gram_local = lax.dot_general(
        panel, panel, (((0,), (0,)), ((), ())), preferred_element_type=jnp.float32
    )
    summed = lax.psum(gram_local, ("wide", "narrow"))
    chol_lower = block_cholesky(summed)
    q_local = solve_right(chol_lower, panel.astype(jnp.float32))
    rotated = lax.psum(
        jnp.dot(targets.astype(jnp.float32), q_local, precision=highest), ("wide", "narrow")
    )
    coefficients = lower_solve(chol_lower, rotated)
    rows_total = panel.shape[0] * lax.axis_size("wide") * lax.axis_size("narrow")
    return (q_local * math.sqrt(rows_total), coefficients)


def solution(mesh):
    placed = (
        P(("wide", "narrow")),
        P(("wide", "narrow")),
        P(("wide", "narrow")),
        P(None, "narrow"),
    )
    return jax.shard_map(
        per_device,
        mesh=mesh,
        in_specs=placed,
        out_specs=(P(("wide", "narrow"), None), P()),
        check_vma=False,
    )
```

profile of v0, /device:TPU:0, one launch (start us, length us, event | category | flops | bytes accessed | tf_op | source)
XLA Modules:
  0.0 1510.9 jit_solution(7513974032531422854)
XLA Ops:
  7.2 14.9 all_gather.7
  22.2 25.3 %gather_fusion = bf16[4096,512]{1,0:T(8,128)(2,1)} fusion(bf16[16384,512]{1,0:T(8,128)(2,1)} %param.28, s32[4096]{0:T(1024)S(1)} %get-tuple-element.308), kind=kCustom, calls=%fused_computation.clone | custom fusion | bytes 8404992 | tf_op jit(solution)/shard_map/jit(_take)/gather | solution.py:26
  47.5 25.3 %gather_fusion.1 = bf16[4096,512]{1,0:T(8,128)(2,1)} fusion(bf16[16384,512]{1,0:T(8,128)(2,1)} %param.28, s32[4096]{0:T(1024)S(1)} %get-tuple-element.309), kind=kCustom, calls=%fused_computation.1.clone | custom fusion | bytes 8404992 | tf_op jit(solution)/shard_map/jit(_take)/gather | solution.py:26
  72.9 25.3 %gather_fusion.2 = bf16[4096,512]{1,0:T(8,128)(2,1)} fusion(bf16[16384,512]{1,0:T(8,128)(2,1)} %param.28, s32[4096]{0:T(1024)S(1)} %get-tuple-element.310), kind=kCustom, calls=%fused_computation.2.clone | custom fusion | bytes 8404992 | tf_op jit(solution)/shard_map/jit(_take)/gather | solution.py:26
  98.2 25.4 %gather_fusion.3 = bf16[4096,512]{1,0:T(8,128)(2,1)} fusion(bf16[16384,512]{1,0:T(8,128)(2,1)} %param.28, s32[4096]{0:T(1024)S(1)} %get-tuple-element.311), kind=kCustom, calls=%fused_computation.3.clone | custom fusion | bytes 8404992 | tf_op jit(solution)/shard_map/jit(_take)/gather | solution.py:26
  123.6 13.1 all_gather.6
  145.1 92.0 %all_to_all.19 = bf16[4,1024,512]{2,1,0:T(8,128)(2,1)S(1)} all-to-all(bf16[4,1024,512]{2,1,0:T(8,128)(2,1)S(1)} %bitcast.495), channel_id=1, replica_groups=mesh['wide'=8,'narrow'=4] {'narrow'}, dimensions={0} | all-to-all | bytes 8388608 | tf_op jit(solution)/shard_map/all_to_all | solution.py:110
  259.2 269.9 %all-reduce.4.cloned.1.call-done = f32[2048,2048]{0,1:T(8,128)} async-done(((f32[2048,2048]{0,1:T(8,128)}), f32[2048,2048]{0,1:T(8,128)}) %all-reduce.4.cloned.1.call-update) | async-done | bytes 16777232 | tf_op jit(solution)/shard_map/psum | solution.py:114
  599.9 11.9 cholesky.519
  624.1 39.3 %custom-call.32 = f32[4,128,128]{1,2,0:T(8,128)S(1)} custom-call(f32[4,128,128]{2,1,0:T(8,128)S(1)} %get-tuple-element.113), custom_call_target="InvertDiagBlocksLowerTriangular" | custom-call | tf_op jit(solution)/shard_map/triangular_solve | solution.py:52
  790.6 39.7 %custom-call.56 = f32[4,128,128]{1,2,0:T(8,128)S(1)} custom-call(f32[4,128,128]{2,1,0:T(8,128)S(1)} %get-tuple-element.164), custom_call_target="InvertDiagBlocksLowerTriangular" | custom-call | tf_op jit(solution)/shard_map/triangular_solve/custom-call.8 | solution.py:52
  849.9 11.8 copy.113
  890.6 12.1 cholesky.625
  937.3 11.9 cholesky.663
  961.2 39.3 %custom-call.33 = f32[4,128,128]{1,2,0:T(8,128)S(1)} custom-call(f32[4,128,128]{2,1,0:T(8,128)S(1)} %get-tuple-element.121), custom_call_target="InvertDiagBlocksLowerTriangular" | custom-call | tf_op jit(solution)/shard_map/triangular_solve | solution.py:52
  1121.3 39.9 %custom-call.66 = f32[4,128,128]{1,2,0:T(8,128)} custom-call(f32[4,128,128]{2,1,0:T(8,128)S(1)} %get-tuple-element.168), custom_call_target="InvertDiagBlocksLowerTriangular" | custom-call | tf_op jit(solution)/shard_map/triangular_solve/custom-call.8 | solution.py:73
  1169.7 39.3 %custom-call.60 = f32[4,128,128]{1,2,0:T(8,128)S(1)} custom-call(f32[4,128,128]{2,1,0:T(8,128)S(1)} %get-tuple-element.165), custom_call_target="InvertDiagBlocksLowerTriangular" | custom-call | tf_op jit(solution)/shard_map/triangular_solve/custom-call.8 | solution.py:73
  1231.1 12.0 while.31
  1243.1 39.5 %custom-call.61 = f32[4,128,128]{1,2,0:T(8,128)S(1)} custom-call(f32[4,128,128]{2,1,0:T(8,128)S(1)} %get-tuple-element.166), custom_call_target="InvertDiagBlocksLowerTriangular" | custom-call | tf_op jit(solution)/shard_map/triangular_solve/custom-call.8 | solution.py:73
  1297.6 16.6 %slice_subtract_fusion.1 = f32[1024,512]{1,0:T(8,128)} fusion(f32[1024,2048]{1,0:T(8,128)} %convert_element_type.28, f32[2048,2048]{1,0:T(8,128)} %fusion.189, f32[1024,128]{0,1:T(8,128)S(1)} %fusion.296, f32[1024,128]{0,1:T(8,128)S(1)} %fusion.295, f32[1024,128]{0,1:T(8,128)S(1)} %fusion.294, f32[1024,128]{0,1:T(8,128)S(1)} %bitcast.498, ...), kind=kOutput, calls=%fused_computation.79 | convolution fusion | flops 6450315264 | bytes 10485760 | tf_op jit(solution)/shard_map/dot_general | solution.py:69
  1314.2 11.7 while.32
  1326.0 40.2 %custom-call.62 = f32[4,128,128]{1,2,0:T(8,128)} custom-call(f32[4,128,128]{2,1,0:T(8,128)S(1)} %get-tuple-element.167), custom_call_target="InvertDiagBlocksLowerTriangular" | custom-call | tf_op jit(solution)/shard_map/triangular_solve/custom-call.8 | solution.py:73
  1380.4 24.3 %slice_subtract_fusion = f32[1024,512]{1,0:T(8,128)} fusion(f32[1024,2048]{1,0:T(8,128)} %convert_element_type.28, f32[2048,2048]{1,0:T(8,128)} %fusion.189, f32[1024,128]{0,1:T(8,128)} %fusion.299, f32[1024,128]{0,1:T(8,128)} %copy-done.8, f32[1024,128]{0,1:T(8,128)} %copy-done.3, f32[1024,128]{0,1:T(8,128)S(1)} %bitcast.503, f32[1024,128]{0,1:T(8,128)} %copy-done.18, ...), kind=kOutput, calls=%fused_computation.77 | convolution fusion | flops 9681502208 | bytes 13631488 | tf_op jit(solution)/shard_map/dot_general | solution.py:69
  1430.1 40.2 %psum.15 = f32[2048]{0:T(1024)S(1)} all-reduce(f32[2048]{0:T(1024)S(1)} %bitcast.511), channel_id=1, replica_groups=mesh['wide'=8,'narrow'=4] {'wide','narrow'}, use_global_device_ids=true, to_apply=%region_9.0 | all-reduce | flops 2048 | bytes 16384 | tf_op jit(solution)/shard_map/psum | solution.py:117
  (399 shorter events, 627.7 us)
Async XLA Ops:
  7.2 521.9 %all-reduce.4.cloned.1.call-start = ((), (), s32[]{:S(2)}) async-start(), calls=%async_computation.1 | async-start | bytes 33554432 | tf_op jit(solution)/shard_map/psum | solution.py:114
  98.2 25.4 %copy-start.36 = (s32[1024]{0:T(1024)S(1)}, s32[1024]{0:T(1024)}, u32[]{:S(2)}) copy-start(s32[1024]{0:T(1024)} %param.26) | copy-start | bytes 12292
  624.1 41.4 %copy-start.15 = (f32[512,512]{1,0:T(8,128)}, f32[512,512]{1,0:T(8,128)S(1)}, u32[]{:S(2)}) copy-start(f32[512,512]{1,0:T(8,128)S(1)} %get-tuple-element.638) | copy-start | bytes 3145732
  681.9 7.9 copy-start.12
  681.9 7.9 copy-start.13
  681.9 7.9 copy-start.14
  790.6 39.7 %copy-start.16 = (f32[512,512]{1,0:T(8,128)}, f32[512,512]{1,0:T(8,128)S(1)}, u32[]{:S(2)}) copy-start(f32[512,512]{1,0:T(8,128)S(1)} %get-tuple-element.640) | copy-start | bytes 3145732
  1009.5 5.6 copy-start.27
  1121.2 95.6 %copy-start.10 = (f32[512,512]{1,0:T(8,128)}, f32[512,512]{1,0:T(8,128)S(1)}, u32[]{:S(2)}) copy-start(f32[512,512]{1,0:T(8,128)S(1)} %get-tuple-element.634) | copy-start | bytes 3145732
  1169.7 43.7 %copy-start.11 = (f32[512,512]{1,0:T(8,128)}, f32[512,512]{1,0:T(8,128)S(1)}, u32[]{:S(2)}) copy-start(f32[512,512]{1,0:T(8,128)S(1)} %get-tuple-element.635) | copy-start | bytes 3145732
  1221.3 76.2 %copy-start.6 = (f32[1024,128]{0,1:T(8,128)}, f32[1024,128]{0,1:T(8,128)S(1)}, u32[]{:S(2)}) copy-start(f32[1024,128]{0,1:T(8,128)S(1)} %fusion.293) | copy-start | bytes 1572868
  1292.3 21.9 %copy-start.7 = (f32[1024,128]{0,1:T(8,128)}, f32[1024,128]{0,1:T(8,128)S(1)}, u32[]{:S(2)}) copy-start(f32[1024,128]{0,1:T(8,128)S(1)} %fusion.295) | copy-start | bytes 1572868
  1297.5 16.6 %copy-start.18 = (f32[1024,128]{0,1:T(8,128)}, f32[1024,128]{0,1:T(8,128)S(1)}, u32[]{:S(2)}) copy-start(f32[1024,128]{0,1:T(8,128)S(1)} %fusion.296) | copy-start | bytes 1572868
  1366.1 8.3 copy-start.25
  1404.7 8.4 copy-start.21
  1408.6 10.3 copy-start.4
  1410.2 7.3 copy-start.5
  1426.0 44.3 %copy-start.22 = (f32[4,128,128]{1,2,0:T(8,128)S(1)}, f32[4,128,128]{1,2,0:T(8,128)}, u32[]{:S(2)}) copy-start(f32[4,128,128]{1,2,0:T(8,128)} %custom-call.66) | copy-start | bytes 786436
  1426.0 48.4 %copy-start.28 = (f32[512,128]{1,0:T(8,128)S(1)}, f32[512,128]{1,0:T(8,128)}, u32[]{:S(2)}) copy-start(f32[512,128]{1,0:T(8,128)} %copy-done.27) | copy-start | bytes 786436
  1426.0 48.4 %copy-start.30 = (f32[512,128]{1,0:T(8,128)S(1)}, f32[512,128]{1,0:T(8,128)}, u32[]{:S(2)}) copy-start(f32[512,128]{1,0:T(8,128)} %copy-done.29) | copy-start | bytes 786436
  1426.0 48.4 %copy-start.32 = (f32[512,128]{1,0:T(8,128)S(1)}, f32[512,128]{1,0:T(8,128)}, u32[]{:S(2)}) copy-start(f32[512,128]{1,0:T(8,128)} %copy-done.31) | copy-start | bytes 786436
  1426.0 48.4 %copy-start.34 = (f32[512,128]{1,0:T(8,128)S(1)}, f32[512,128]{1,0:T(8,128)}, u32[]{:S(2)}) copy-start(f32[512,128]{1,0:T(8,128)} %copy-done.33) | copy-start | bytes 786436
  1426.0 49.1 %copy-start.26 = (f32[4,128,128]{1,2,0:T(8,128)S(1)}, f32[4,128,128]{1,2,0:T(8,128)}, u32[]{:S(2)}) copy-start(f32[4,128,128]{1,2,0:T(8,128)} %custom-call.62) | copy-start | bytes 786436
  1430.1 52.0 %copy-start.24 = (f32[4,128,128]{1,2,0:T(8,128)S(1)}, f32[4,128,128]{1,2,0:T(8,128)}, u32[]{:S(2)}) copy-start(f32[4,128,128]{1,2,0:T(8,128)} %copy-done.23) | copy-start | bytes 786436
  (15 other events, 46.3 us)
Sparse Core Ops, SparseCore 0:
  251.6 277.4 all-reduce.3
where the time goes:
time: 1530 us; the launch traced here: 1510 us
  other arithmetic  632 us (41%)
  waiting for transfers between devices  270 us (18%)
  matrix products  216 us (14%)
  local copies, waits for them, and re-layouts  207 us (14%)
  blocking collectives  160 us (10%)
  between operations  25.6 us (2%)
    another operation x59, other arithmetic, block_cholesky(): diag_factor = jnp.linalg.cholesky(diag_block)  317 us
    psum x1, waiting for transfers between devices, per_device(): summed = lax.psum(gram_local, ('wide', 'narrow'))  270 us
    another operation x6, other arithmetic, solve_right(): lax.linalg.triangular_solve(chol_lower[low:high, low:high], rhs_block, le...  163 us
    another operation x8, other arithmetic, block_cholesky(): lax.linalg.triangular_solve(diag_factor, below, left_side=False, lower=Tr...  123 us
    gather x4, local copies, waits for them, and re-layouts, project(): jnp.take(basis_cols, start_point + offset, axis=0).astype(jnp.float32)  101 us
    all_to_all x1, blocking collectives, per_device(): lax.all_to_all(columns, 'narrow', split_axis=0, concat_axis=1, tiled=True)  92 us
    another operation x28, matrix products, solve_right(): lax.linalg.triangular_solve(chol_lower[low:high, low:high], rhs_block, le...  55.3 us
    dot_general x3, matrix products, solve_right(): jnp.dot(earlier, chol_lower[low:high, :low].T, precision=highest)  50.7 us
  transfers between devices with their start and end apart: 1, of which 1 were waited for; matrix products, arithmetic and copies ran while one was open for 0% of the time, Pallas kernels for 0%

commit v1 on v0

v1 whole, which is shorter than its diff:
```python
import functools
import math

import jax
import jax.numpy as jnp
from jax import lax
from jax.experimental import pallas as pl
from jax.experimental.pallas import tpu as pltpu
from jax.sharding import PartitionSpec as P

VMEM = 56 * 1024 * 1024
LEAF = 128
nt = (((1,), (1,)), ((), ()))
nn = (((1,), (0,)), ((), ()))


def split(value):
    high = value.astype(jnp.bfloat16)
    low = (value - high.astype(jnp.float32)).astype(jnp.bfloat16)
    return high, low


def dot3(left, right, dims):
    def one(a, b):
        return lax.dot_general(a, b, dims, preferred_element_type=jnp.float32)

    return one(left[0], right[0]) + (one(left[0], right[1]) + one(left[1], right[0]))


def lane_spread(value, lane):
    return jnp.broadcast_to(value[:, lane : lane + 1], value.shape)


def row_spread(value, row):
    return jnp.broadcast_to(value[row : row + 1, :], value.shape)


def reciprocal(value):
    guess = pltpu.reciprocal(value, approx=True)
    return guess * (2.0 - value * guess)


def invert_leaf(m):
    size = m.shape[0]
    row_at = lax.broadcasted_iota(jnp.int32, (8, size), 0)
    lane_at = lax.broadcasted_iota(jnp.int32, (8, size), 1)
    for step in range(size // 8):
        low = 8 * step
        own = m[low : low + 8, :]
        columns = [lane_spread(own, low + j) for j in range(8)]
        inside = (lane_at >= low) & (lane_at < low + 8)
        own = jnp.where(inside, jnp.where(lane_at - low == row_at, 1.0, 0.0), own)
        pivots = jnp.ones_like(own)
        factors, inverses, rows = {}, [], []
        for j in range(8):
            pivot = row_spread(columns[j], j)
            inverse = reciprocal(pivot)
            inverses.append(inverse)
            pivots = jnp.where(row_at == j, pivot, pivots)
            rows.append(row_spread(own, j))
            if j < 7:
                scaled = jnp.where(row_at > j, columns[j] * inverse, 0.0)
                for other in range(j + 1, 8):
                    factors[j, other] = row_spread(columns[other], j)
                    columns[other] = columns[other] - scaled * factors[j, other]
                own = own - scaled * rows[j]
        for group in range(step + 1, size // 8):
            below = m[8 * group : 8 * group + 8, :]
            columns = [lane_spread(below, low + j) for j in range(8)]
            below = jnp.where(inside, 0.0, below)
            for j in range(8):
                scaled = columns[j] * inverses[j]
                for other in range(j + 1, 8):
                    columns[other] = columns[other] - scaled * factors[j, other]
                below = below - scaled * rows[j]
            m[8 * group : 8 * group + 8, :] = below
        m[low : low + 8, :] = jnp.where(lane_at < low + 8, own * lax.rsqrt(pivots), 0.0)


def invert_block(d, m):
    size = d.shape[0]
    for step in range(size // LEAF):
        low, high = step * LEAF, (step + 1) * LEAF
        m[...] = d[low:high, low:high]
        invert_leaf(m)
        leaf = split(m[...])
        pieces = [m[...]]
        if low:
            pieces.insert(0, dot3(leaf, split(d[low:high, :low]), nn))
        if high < size:
            ahead = dot3(leaf, split(d[low:high, high:]), nn)
            factor = split(dot3(split(d[high:, low:high]), leaf, nt))
            d[high:, low:high] = -dot3(factor, leaf, nn)
            d[high:, high:] = d[high:, high:] - dot3(factor, split(ahead), nn)
            if low:
                d[high:, :low] = d[high:, :low] - dot3(factor, split(pieces[0]), nn)
            pieces.append(jnp.zeros_like(ahead))
        d[low:high, :] = jnp.concatenate(pieces, axis=1)


def stage_kernel(stage, width, below, *refs):
    gram_ref = refs[0]
    earlier = [(refs[1 + 2 * k], refs[2 + 2 * k]) for k in range(stage)]
    refs = refs[1 + 2 * stage :]
    inv_high, inv_low = refs[:2]
    d, m = refs[-2:]

    def rows_of(k, first, count):
        at = pl.ds(first + (stage - k - 1) * width, count)
        return earlier[k][0][at, :], earlier[k][1][at, :]

    total = gram_ref[:width, :]
    for k in range(stage):
        own = rows_of(k, 0, width)
        total = total - dot3(own, own, nt)
    d[...] = total
    invert_block(d, m)
    high, low = split(d[...])
    inv_high[...] = high
    inv_low[...] = low
    if below:
        out_high, out_low = refs[2:4]
        tile = width // 2

        def body(index, carry):
            first = pl.multiple_of(index * tile, tile)
            value = gram_ref[pl.ds(width + first, tile), :]
            for k in range(stage):
                value = value - dot3(rows_of(k, width + first, tile), rows_of(k, 0, width), nt)
            value = dot3(split(value), (inv_high[...], inv_low[...]), nt)
            out_high[pl.ds(first, tile), :], out_low[pl.ds(first, tile), :] = split(value)
            return carry

        lax.fori_loop(0, below // tile, body, 0)


def factor_stage(stage, gram_columns, earlier):
    rows, width = gram_columns.shape
    below = rows - width
    shapes = [jax.ShapeDtypeStruct((width, width), jnp.bfloat16)] * 2
    if below:
        shapes += [jax.ShapeDtypeStruct((below, width), jnp.bfloat16)] * 2
    flat = [part for pair in earlier for part in pair]
    out = pl.pallas_call(
        functools.partial(stage_kernel, stage, width, below),
        out_shape=shapes,
        in_specs=[pl.BlockSpec(memory_space=pltpu.VMEM)] * (1 + len(flat)),
        out_specs=[pl.BlockSpec(memory_space=pltpu.VMEM)] * len(shapes),
        scratch_shapes=[pltpu.VMEM((width, width), jnp.float32), pltpu.VMEM((LEAF, LEAF), jnp.float32)],
        compiler_params=pltpu.CompilerParams(vmem_limit_bytes=VMEM),
        name="factor",
    )(gram_columns, *flat)
    return tuple(out[:2]), tuple(out[2:])


def q_kernel(count, scale, panel_ref, *refs):
    inverses = [(refs[2 * k], refs[2 * k + 1]) for k in range(count)]
    lowers = [(refs[2 * (count + k)], refs[2 * (count + k) + 1]) for k in range(count - 1)]
    out_ref = refs[-1]
    width = inverses[0][0].shape[0]
    done = []
    for stage in range(count):
        columns = slice(stage * width, (stage + 1) * width)
        inverse = (inverses[stage][0][...], inverses[stage][1][...])
        value = panel_ref[:, columns]
        if stage:
            value = value.astype(jnp.float32)
            for k in range(stage):
                at = pl.ds((stage - k - 1) * width, width)
                value = value - dot3(done[k], (lowers[k][0][at, :], lowers[k][1][at, :]), nt)
            value = dot3(split(value), inverse, nt)
        else:
            value = sum(
                lax.dot_general(value, part, nt, preferred_element_type=jnp.float32) for part in inverse[::-1]
            )
        out_ref[:, columns] = value * scale
        if stage + 1 < count:
            done.append(split(value))


def solve_panel(panel, inverses, lowers, scale):
    rows, order = panel.shape
    count = len(inverses)
    flat = [part for pair in inverses + lowers for part in pair]
    tile = min(rows, 256)
    return pl.pallas_call(
        functools.partial(q_kernel, count, scale),
        grid=(rows // tile,),
        out_shape=jax.ShapeDtypeStruct((rows, order), jnp.float32),
        in_specs=[pl.BlockSpec((tile, order), lambda i: (i, 0))]
        + [pl.BlockSpec(memory_space=pltpu.VMEM)] * len(flat),
        out_specs=pl.BlockSpec((tile, order), lambda i: (i, 0)),
        compiler_params=pltpu.CompilerParams(vmem_limit_bytes=VMEM),
        name="solve_panel",
    )(panel, *flat)


def coefficient_kernel(count, rhs_ref, *refs):
    inverses = [(refs[2 * k], refs[2 * k + 1]) for k in range(count)]
    lowers = [(refs[2 * (count + k)], refs[2 * (count + k) + 1]) for k in range(count - 1)]
    out_ref = refs[-1]
    width = inverses[0][0].shape[0]

    def lower_at(row, column):
        at = pl.ds((row - column - 1) * width, width)
        return lowers[column][0][at, :], lowers[column][1][at, :]

    def inverse_at(stage):
        return inverses[stage][0][...], inverses[stage][1][...]

    rotated = []
    for stage in range(count):
        value = rhs_ref[:, stage * width : (stage + 1) * width]
        for k in range(stage):
            value = value - dot3(rotated[k], lower_at(stage, k), nt)
        value = dot3(split(value), inverse_at(stage), nt)
        rotated.append(split(value))
    solved = {}
    for stage in reversed(range(count)):
        value = rotated[stage][0].astype(jnp.float32) + rotated[stage][1].astype(jnp.float32)
        for later in range(stage + 1, count):
            value = value - dot3(solved[later], lower_at(later, stage), nn)
        value = dot3(split(value), inverse_at(stage), nn)
        solved[stage] = split(value)
        out_ref[:, stage * width : (stage + 1) * width] = value


def solve_coefficients(rhs, inverses, lowers):
    flat = [part for pair in inverses + lowers for part in pair]
    return pl.pallas_call(
        functools.partial(coefficient_kernel, len(inverses)),
        out_shape=jax.ShapeDtypeStruct(rhs.shape, jnp.float32),
        in_specs=[pl.BlockSpec(memory_space=pltpu.VMEM)] * (1 + len(flat)),
        out_specs=pl.BlockSpec(memory_space=pltpu.VMEM),
        compiler_params=pltpu.CompilerParams(vmem_limit_bytes=VMEM),
        name="coefficients",
    )(rhs, *flat)


def spline_weights(frac_step):
    position = frac_step.astype(jnp.float32) / 64.0
    first = (1.0 - position) ** 3 / 6.0
    second = (3.0 * position**3 - 6.0 * position**2 + 4.0) / 6.0
    third = (-3.0 * position**3 + 3.0 * position**2 + 3.0 * position + 1.0) / 6.0
    fourth = position**3 / 6.0
    return [first, second, third, fourth]


def project(basis_cols, start_point, frac_step):
    weights = spline_weights(frac_step)
    accumulated = jnp.zeros((start_point.shape[0], basis_cols.shape[1]), jnp.float32)
    for offset in range(4):
        picked = jnp.take(basis_cols, start_point + offset, axis=0).astype(jnp.float32)
        accumulated = accumulated + weights[offset][:, None] * picked
    return accumulated.astype(jnp.bfloat16)


def per_device(start_point, frac_step, targets, basis_cols):
    group_start, group_frac = (
        lax.all_gather(start_point, "narrow", axis=0, tiled=True),
        lax.all_gather(frac_step, "narrow", axis=0, tiled=True),
    )
    columns = project(basis_cols, group_start, group_frac)
    panel = lax.all_to_all(columns, "narrow", split_axis=0, concat_axis=1, tiled=True)
    order = panel.shape[1]
    weighted = jnp.concatenate([panel, jnp.broadcast_to(targets[:, None], (panel.shape[0], 8))], axis=1)
    gram_local = lax.dot_general(
        weighted, panel, (((0,), (0,)), ((), ())), preferred_element_type=jnp.float32
    )
    summed = lax.psum(gram_local, ("wide", "narrow"))
    width = min(order, 512)
    inverses, lowers = [], []
    for stage in range(order // width):
        low = stage * width
        inverse, below = factor_stage(stage, summed[low:order, low : low + width], lowers)
        inverses.append(inverse)
        if below:
            lowers.append(below)
    rows_total = panel.shape[0] * lax.axis_size("wide") * lax.axis_size("narrow")
    q_scaled = solve_panel(panel, inverses, lowers, math.sqrt(rows_total))
    coefficients = solve_coefficients(summed[order:], inverses, lowers)
    return q_scaled, coefficients[0]


def solution(mesh):
    rows_at = P(("wide", "narrow"))
    return jax.shard_map(
        per_device,
        mesh=mesh,
        in_specs=(rows_at, rows_at, rows_at, P(None, "narrow")),
        out_specs=(P(("wide", "narrow"), None), P()),
        check_vma=False,
    )
```

time: 1530 us -> 726 us (0.47)
  other arithmetic: 632 us -> 8.46 us
  matrix products: 216 us -> 11.7 us
  Pallas kernels: 0 us -> 162 us
  local copies, waits for them, and re-layouts: 207 us -> 121 us
  blocking collectives: 160 us -> 120 us
    another operation x73 -> x0, other arithmetic: 603 us -> none  [the longest x59 317 us: block_cholesky(): diag_factor = jnp.linalg.cholesky(diag_block)]
    pallas_call x0 -> x6, Pallas kernels: none -> 162 us  [the longest x4 126 us: factor_stage(): pl.pallas_call(functools.partial(stage_kernel, stage, width, below), out_...]
    another operation x101 -> x0, matrix products: 113 us -> none  [the longest x28 55.3 us: solve_right(): lax.linalg.triangular_solve(chol_lower[low:high, low:high], rhs_block, le...]
    dot_general x13 -> x1, matrix products: 103 us -> 11.7 us  [per_device(): lax.dot_general(weighted, panel, (((0,), (0,)), ((), ())), preferred_elem...]
    another operation x108 -> x0, local copies, waits for them, and re-layouts: 68 us -> none  [the longest x48 39.9 us: solve_right(): lax.linalg.triangular_solve(chol_lower[low:high, low:high], rhs_block, le...]
    psum x1 -> x0, blocking collectives: 40.2 us -> none  [per_device(): lax.psum(jnp.dot(targets.astype(jnp.float32), q_local, precision=highest)...]
    unnamed x86 -> x4, local copies, waits for them, and re-layouts: 26.5 us -> 1.91 us
where the time goes in v1:
time: 726 us; the launch traced here: 718 us
  waiting for transfers between devices  280 us (39%)
  Pallas kernels  162 us (22%)
  local copies, waits for them, and re-layouts  121 us (17%)
  blocking collectives  120 us (17%)
  between operations  14.5 us (2%)
  matrix products  11.7 us (2%)
  other arithmetic  8.46 us (1%)
    psum x1, waiting for transfers between devices, per_device(): summed = lax.psum(gram_local, ('wide', 'narrow'))  280 us
    pallas_call x4, Pallas kernels, factor_stage(): pl.pallas_call(functools.partial(stage_kernel, stage, width, below), out_...  126 us
    gather x4, local copies, waits for them, and re-layouts, project(): jnp.take(basis_cols, start_point + offset, axis=0).astype(jnp.float32)  101 us
    all_to_all x1, blocking collectives, per_device(): lax.all_to_all(columns, 'narrow', split_axis=0, concat_axis=1, tiled=True)  92.1 us
    pallas_call x1, Pallas kernels, solve_panel(): pl.pallas_call(functools.partial(q_kernel, count, scale), grid=(rows // t...  24 us
    all_gather x1, blocking collectives, per_device(): lax.all_gather(start_point, 'narrow', axis=0, tiled=True)  14.9 us
  transfers between devices with their start and end apart: 1, of which 1 were waited for; matrix products, arithmetic and copies ran while one was open for 0% of the time, Pallas kernels for 0%

profile of v1, /device:TPU:0, one launch (start us, length us, event | category | flops | bytes accessed | tf_op | source)
XLA Modules:
  0.0 717.6 jit_solution(4480387221766181498)
XLA Ops:
  7.2 14.9 %all_gather.7 = s32[4096]{0:T(1024)S(1)} all-gather(s32[1024]{0:T(1024)} %param.6), channel_id=1, replica_groups=mesh['wide'=8,'narrow'=4] {'narrow'}, dimensions={0}, use_global_device_ids=true | all-gather | bytes 20480 | tf_op jit(solution)/shard_map/all_gather | solution.py:260
  22.2 13.3 %all_gather.6 = s32[4096]{0:T(1024)S(1)} all-gather(s32[1024]{0:T(1024)} %param.7), channel_id=1, replica_groups=mesh['wide'=8,'narrow'=4] {'narrow'}, dimensions={0}, use_global_device_ids=true | all-gather | bytes 20480 | tf_op jit(solution)/shard_map/all_gather | solution.py:261
  35.5 25.4 %gather_fusion = bf16[4096,512]{1,0:T(8,128)(2,1)} fusion(bf16[16384,512]{1,0:T(8,128)(2,1)} %param.9, s32[4096]{0:T(1024)S(1)} %get-tuple-element.39), kind=kCustom, calls=%fused_computation.clone | custom fusion | bytes 8404992 | tf_op jit(solution)/shard_map/jit(_take)/gather | solution.py:253
  60.9 25.3 %gather_fusion.1 = bf16[4096,512]{1,0:T(8,128)(2,1)} fusion(bf16[16384,512]{1,0:T(8,128)(2,1)} %param.9, s32[4096]{0:T(1024)S(1)} %get-tuple-element.40), kind=kCustom, calls=%fused_computation.1.clone | custom fusion | bytes 8404992 | tf_op jit(solution)/shard_map/jit(_take)/gather | solution.py:253
  86.2 25.4 %gather_fusion.2 = bf16[4096,512]{1,0:T(8,128)(2,1)} fusion(bf16[16384,512]{1,0:T(8,128)(2,1)} %param.9, s32[4096]{0:T(1024)S(1)} %get-tuple-element.41), kind=kCustom, calls=%fused_computation.2.clone | custom fusion | bytes 8404992 | tf_op jit(solution)/shard_map/jit(_take)/gather | solution.py:253
  111.6 25.4 %gather_fusion.3 = bf16[4096,512]{1,0:T(8,128)(2,1)} fusion(bf16[16384,512]{1,0:T(8,128)(2,1)} %param.9, s32[4096]{0:T(1024)S(1)} %get-tuple-element.42), kind=kCustom, calls=%fused_computation.3.clone | custom fusion | bytes 8404992 | tf_op jit(solution)/shard_map/jit(_take)/gather | solution.py:253
  136.9 8.4 %add_convert_fusion = bf16[4096,512]{1,0:T(8,128)(2,1)S(1)} fusion(bf16[4096,512]{1,0:T(8,128)(2,1)} %gather_fusion.3, bf16[4096,512]{1,0:T(8,128)(2,1)} %gather_fusion.2, bf16[4096,512]{1,0:T(8,128)(2,1)} %gather_fusion.1, bf16[4096,512]{1,0:T(8,128)(2,1)} %gather_fusion, f32[4096]{0:T(1024)S(1)} %get-tuple-element.37, f32[4096]{0:T(1024)S(1)} %get-tuple-element.38, ...), kind=kLoop, calls=%fused_computation.4 | loop fusion | flops 33554432 | bytes 21053440 | tf_op jit(solution)/shard_map/convert_element_type | solution.py:255
  145.3 92.1 %all_to_all.19 = bf16[4,1024,512]{2,1,0:T(8,128)(2,1)S(1)} all-to-all(bf16[4,1024,512]{2,1,0:T(8,128)(2,1)S(1)} %bitcast.9), channel_id=1, replica_groups=mesh['wide'=8,'narrow'=4] {'narrow'}, dimensions={0} | all-to-all | bytes 8388608 | tf_op jit(solution)/shard_map/all_to_all | solution.py:264
  237.4 0.6 copy.8
  238.3 1.9 copy-done
  240.1 11.7 %fusion = f32[2056,2048]{1,0:T(8,128)} fusion(bf16[1024,2048]{1,0:T(8,128)(2,1)S(1)} %bitcast.7, bf16[1024,8]{1,0:T(8,128)(2,1)S(1)} %broadcast_in_dim.11), kind=kOutput, calls=%fused_computation.5 | convolution fusion | flops 8631910400 | bytes 21053440 | tf_op jit(solution)/shard_map/dot_general | solution.py:267
  251.8 280.3 %all-reduce.2.cloned.1.call-done = f32[2056,2048]{1,0:T(8,128)} async-done(((f32[2056,2048]{1,0:T(8,128)}), f32[2056,2048]{1,0:T(8,128)}) %all-reduce.2.cloned.1.call-update) | async-done | bytes 16842768 | tf_op jit(solution)/shard_map/psum | solution.py:270
  532.1 4.6 slice.32.refs_0_
  536.7 38.8 %factor.4 = (bf16[512,512]{1,0:T(8,128)(2,1)}, bf16[512,512]{1,0:T(8,128)(2,1)}, bf16[1536,512]{1,0:T(8,128)(2,1)}, bf16[1536,512]{1,0:T(8,128)(2,1)}) custom-call(f32[2048,512]{1,0:T(8,128)} %slice.32.refs_0_), custom_call_target="tpu_custom_call" | custom-call | tf_op jit(solution)/shard_map/factor/pallas_call | solution.py:144
  575.5 3.9 slice.33.refs_0_
  579.4 30.4 %factor.5 = (bf16[512,512]{1,0:T(8,128)(2,1)}, bf16[512,512]{1,0:T(8,128)(2,1)}, bf16[1024,512]{1,0:T(8,128)(2,1)}, bf16[1024,512]{1,0:T(8,128)(2,1)}) custom-call(f32[1536,512]{1,0:T(8,128)} %slice.33.refs_0_, bf16[1536,512]{1,0:T(8,128)(2,1)} %get-tuple-element.19.refs_1_.refs_8_, bf16[1536,512]{1,0:T(8,128)(2,1)} %get-tuple-element.20.refs_2_.refs_9_), custom_call_target="tpu_custom_call" | custom-call | tf_op jit(solution)/shard_map/factor/pallas_call | solution.py:144
  609.7 3.1 slice.34.refs_0_
  612.8 29.6 %factor.6 = (bf16[512,512]{1,0:T(8,128)(2,1)}, bf16[512,512]{1,0:T(8,128)(2,1)}, bf16[512,512]{1,0:T(8,128)(2,1)}, bf16[512,512]{1,0:T(8,128)(2,1)}) custom-call(f32[1024,512]{1,0:T(8,128)} %slice.34.refs_0_, bf16[1536,512]{1,0:T(8,128)(2,1)} %get-tuple-element.19.refs_1_.refs_8_, bf16[1536,512]{1,0:T(8,128)(2,1)} %get-tuple-element.20.refs_2_.refs_9_, ...), custom_call_target="tpu_custom_call" | custom-call | tf_op jit(solution)/shard_map/factor/pallas_call | solution.py:144
  642.4 2.3 slice.35.refs_0_
  644.6 27.3 %factor.7 = (bf16[512,512]{1,0:T(8,128)(2,1)}, bf16[512,512]{1,0:T(8,128)(2,1)}) custom-call(f32[512,512]{1,0:T(8,128)} %slice.35.refs_0_, bf16[1536,512]{1,0:T(8,128)(2,1)} %get-tuple-element.19.refs_1_.refs_8_, bf16[1536,512]{1,0:T(8,128)(2,1)} %get-tuple-element.20.refs_2_.refs_9_, bf16[1024,512]{1,0:T(8,128)(2,1)} %get-tuple-element.23.refs_3_.refs_10_, ...), custom_call_target="tpu_custom_call" | custom-call | tf_op jit(solution)/shard_map/factor/pallas_call | solution.py:144
  671.9 24.0 %solve_panel.1 = f32[1024,2048]{1,0:T(8,128)} custom-call(bf16[1024,2048]{1,0:T(8,128)(2,1)} %bitcast.8, bf16[512,512]{1,0:T(8,128)(2,1)} %get-tuple-element.17.refs_0_, bf16[512,512]{1,0:T(8,128)(2,1)} %get-tuple-element.18.refs_1_, bf16[512,512]{1,0:T(8,128)(2,1)} %get-tuple-element.21.refs_2_, bf16[512,512]{1,0:T(8,128)(2,1)} %get-tuple-element.22.refs_3_, ...), custom_call_target="tpu_custom_call" | custom-call | tf_op jit(solution)/shard_map/solve_panel/pallas_call | solution.py:186
  695.9 1.5 slice.36.rhs_ref
  697.3 11.6 %coefficients.1 = f32[8,2048]{1,0:T(8,128)} custom-call(f32[8,2048]{1,0:T(8,128)} %slice.36.rhs_ref, bf16[512,512]{1,0:T(8,128)(2,1)} %get-tuple-element.17.refs_0_, bf16[512,512]{1,0:T(8,128)(2,1)} %get-tuple-element.18.refs_1_, bf16[512,512]{1,0:T(8,128)(2,1)} %get-tuple-element.21.refs_2_, bf16[512,512]{1,0:T(8,128)(2,1)} %get-tuple-element.22.refs_3_, ...), custom_call_target="tpu_custom_call" | custom-call | tf_op jit(solution)/shard_map/coefficients/pallas_call | solution.py:230
  708.9 1.4 slice.37
  (9 shorter events, 0.4 us)
Async XLA Ops:
  7.2 524.9 %all-reduce.2.cloned.1.call-start = ((), (), s32[]{:S(2)}) async-start(), calls=%async_computation.1 | async-start | bytes 33685504 | tf_op jit(solution)/shard_map/psum | solution.py:270
  237.4 0.7 copy-start.1
  238.1 2.1 copy-start
Sparse Core Ops, SparseCore 0:
  252.0 280.1 all-reduce.1

commit v2 on v1

v2 whole, which is shorter than its diff:
```python
import functools
import math

import jax
import jax.numpy as jnp
from jax import lax
from jax.experimental import pallas as pl
from jax.experimental.pallas import tpu as pltpu
from jax.sharding import PartitionSpec as P

VMEM = 56 * 1024 * 1024
LEAF = 128
nt = (((1,), (1,)), ((), ()))
nn = (((1,), (0,)), ((), ()))


def split(value):
    high = value.astype(jnp.bfloat16)
    low = (value - high.astype(jnp.float32)).astype(jnp.bfloat16)
    return high, low


def dot3(left, right, dims):
    def one(a, b):
        return lax.dot_general(a, b, dims, preferred_element_type=jnp.float32)

    return one(left[0], right[0]) + (one(left[0], right[1]) + one(left[1], right[0]))


def lane_spread(value, lane):
    return jnp.broadcast_to(value[:, lane : lane + 1], value.shape)


def row_spread(value, row):
    return jnp.broadcast_to(value[row : row + 1, :], value.shape)


def reciprocal(value):
    guess = pltpu.reciprocal(value, approx=True)
    return guess * (2.0 - value * guess)


def invert_leaf(m):
    size = m.shape[0]
    row_at = lax.broadcasted_iota(jnp.int32, (8, size), 0)
    lane_at = lax.broadcasted_iota(jnp.int32, (8, size), 1)
    for step in range(size // 8):
        low = 8 * step
        own = m[low : low + 8, :]
        columns = [lane_spread(own, low + j) for j in range(8)]
        inside = (lane_at >= low) & (lane_at < low + 8)
        own = jnp.where(inside, jnp.where(lane_at - low == row_at, 1.0, 0.0), own)
        pivots = jnp.ones_like(own)
        factors, inverses, rows = {}, [], []
        for j in range(8):
            pivot = row_spread(columns[j], j)
            inverse = reciprocal(pivot)
            inverses.append(inverse)
            pivots = jnp.where(row_at == j, pivot, pivots)
            rows.append(row_spread(own, j))
            if j < 7:
                scaled = jnp.where(row_at > j, columns[j] * inverse, 0.0)
                for other in range(j + 1, 8):
                    factors[j, other] = row_spread(columns[other], j)
                    columns[other] = columns[other] - scaled * factors[j, other]
                own = own - scaled * rows[j]
        for group in range(step + 1, size // 8):
            below = m[8 * group : 8 * group + 8, :]
            columns = [lane_spread(below, low + j) for j in range(8)]
            below = jnp.where(inside, 0.0, below)
            for j in range(8):
                scaled = columns[j] * inverses[j]
                for other in range(j + 1, 8):
                    columns[other] = columns[other] - scaled * factors[j, other]
                below = below - scaled * rows[j]
            m[8 * group : 8 * group + 8, :] = below
        m[low : low + 8, :] = jnp.where(lane_at < low + 8, own * lax.rsqrt(pivots), 0.0)


def invert_block(d, m):
    size = d.shape[0]
    for step in range(size // LEAF):
        low, high = step * LEAF, (step + 1) * LEAF
        m[...] = d[low:high, low:high]
        invert_leaf(m)
        leaf = split(m[...])
        pieces = [m[...]]
        if low:
            pieces.insert(0, dot3(leaf, split(d[low:high, :low]), nn))
        if high < size:
            ahead = dot3(leaf, split(d[low:high, high:]), nn)
            factor = split(dot3(split(d[high:, low:high]), leaf, nt))
            d[high:, low:high] = -dot3(factor, leaf, nn)
            d[high:, high:] = d[high:, high:] - dot3(factor, split(ahead), nn)
            if low:
                d[high:, :low] = d[high:, :low] - dot3(factor, split(pieces[0]), nn)
            pieces.append(jnp.zeros_like(ahead))
        d[low:high, :] = jnp.concatenate(pieces, axis=1)


def read_pair(pair, first, count):
    at = pl.ds(first, count)
    return pair[0][at, :], pair[1][at, :]


def invert_kernel(stage, diag_ref, *refs):
    earlier = [(refs[2 * k], refs[2 * k + 1]) for k in range(stage)]
    inv_high, inv_low, d, m = refs[2 * stage :]
    slices, rows, width = diag_ref.shape
    count = width // slices
    for piece in range(slices):
        d[piece * count : (piece + 1) * count, :] = diag_ref[piece, :count, :]
    for k in range(stage):
        own = read_pair(earlier[k], (stage - k - 1) * width, width)
        d[...] = d[...] - dot3(own, own, nt)
    invert_block(d, m)
    inv_high[...], inv_low[...] = split(d[...])


def invert_stage(stage, diagonal, slot, earlier):
    slices, _, rows, width = diagonal.shape
    flat = [part for pair in earlier for part in pair]
    whole = pl.BlockSpec(memory_space=pltpu.VMEM)
    return pl.pallas_call(
        functools.partial(invert_kernel, stage),
        grid=(1,),
        out_shape=[jax.ShapeDtypeStruct((width, width), jnp.bfloat16)] * 2,
        in_specs=[pl.BlockSpec((slices, None, rows, width), lambda i: (0, slot, 0, 0))] + [whole] * len(flat),
        out_specs=[whole] * 2,
        scratch_shapes=[pltpu.VMEM((width, width), jnp.float32), pltpu.VMEM((LEAF, LEAF), jnp.float32)],
        compiler_params=pltpu.CompilerParams(vmem_limit_bytes=VMEM),
        cost_estimate=pl.CostEstimate(flops=25_000_000_000 if stage else 1_000_000, bytes_accessed=4 * width * width, transcendentals=0),
        name="invert_diagonal",
    )(diagonal, *flat)


def below_kernel(stage, offset, off_ref, inv_high, inv_low, *refs):
    earlier = [(refs[2 * k], refs[2 * k + 1]) for k in range(stage)]
    out_high, out_low = refs[2 * stage :]
    below, width = out_high.shape
    tile = width // 2

    def body(index, carry):
        first = pl.multiple_of(index * tile, tile)
        value = off_ref[pl.ds(offset + first, tile), :].astype(jnp.float32)
        for k in range(stage):
            skip = (stage - k - 1) * width
            value = value - dot3(
                read_pair(earlier[k], skip + width + first, tile), read_pair(earlier[k], skip, width), nt
            )
        value = dot3(split(value), (inv_high[...], inv_low[...]), nt)
        out_high[pl.ds(first, tile), :], out_low[pl.ds(first, tile), :] = split(value)
        return carry

    lax.fori_loop(0, below // tile, body, 0)


def below_stage(stage, below, off_diagonal, offset, inverse, earlier):
    width = off_diagonal.shape[1]
    flat = [part for pair in earlier for part in pair]
    whole = pl.BlockSpec(memory_space=pltpu.VMEM)
    return pl.pallas_call(
        functools.partial(below_kernel, stage, offset),
        out_shape=[jax.ShapeDtypeStruct((below, width), jnp.bfloat16)] * 2,
        in_specs=[whole] * (3 + len(flat)),
        out_specs=[whole] * 2,
        compiler_params=pltpu.CompilerParams(vmem_limit_bytes=VMEM),
        cost_estimate=pl.CostEstimate(
            flops=6 * below * width * width * (stage + 1), bytes_accessed=8 * below * width, transcendentals=0
        ),
        name="factor_below",
    )(off_diagonal, *inverse, *flat)


def q_kernel(count, scale, panel_ref, rhs_ref, *refs):
    inverses = [(refs[2 * k], refs[2 * k + 1]) for k in range(count)]
    lowers = [(refs[2 * (count + k)], refs[2 * (count + k) + 1]) for k in range(count - 1)]
    out_ref, coefficients_ref, rotated = refs[-3:]
    width = inverses[0][0].shape[0]
    rows = panel_ref.shape[0]
    done = []
    for stage in range(count):
        columns = slice(stage * width, (stage + 1) * width)
        inverse = (inverses[stage][0][...], inverses[stage][1][...])
        value = jnp.concatenate([panel_ref[:, columns].astype(jnp.float32), rhs_ref[:, columns]], axis=0)
        for k in range(stage):
            value = value - dot3(done[k], read_pair(lowers[k], (stage - k - 1) * width, width), nt)
        value = dot3(split(value), inverse, nt)
        out_ref[:, columns] = value[:rows] * scale
        rotated[:, columns] = value[rows:]
        if stage + 1 < count:
            done.append(split(value))

    @pl.when(pl.program_id(0) == 0)
    def _():
        solved = {}
        for stage in reversed(range(count)):
            columns = slice(stage * width, (stage + 1) * width)
            value = rotated[:, columns]
            for later in range(stage + 1, count):
                value = value - dot3(solved[later], read_pair(lowers[stage], (later - stage - 1) * width, width), nn)
            value = dot3(split(value), (inverses[stage][0][...], inverses[stage][1][...]), nn)
            solved[stage] = split(value)
            coefficients_ref[:, columns] = value[:1]


def solve_panel(panel, rhs, inverses, lowers, scale):
    rows, order = panel.shape
    count = len(inverses)
    flat = [part for pair in inverses + lowers for part in pair]
    tile = min(rows, 256)
    return pl.pallas_call(
        functools.partial(q_kernel, count, scale),
        grid=(rows // tile,),
        out_shape=[
            jax.ShapeDtypeStruct((rows, order), jnp.float32),
            jax.ShapeDtypeStruct((1, order), jnp.float32),
        ],
        in_specs=[pl.BlockSpec((tile, order), lambda i: (i, 0))]
        + [pl.BlockSpec(memory_space=pltpu.VMEM)] * (1 + len(flat)),
        out_specs=[pl.BlockSpec((tile, order), lambda i: (i, 0)), pl.BlockSpec((1, order), lambda i: (0, 0))],
        scratch_shapes=[pltpu.VMEM((rhs.shape[0], order), jnp.float32)],
        compiler_params=pltpu.CompilerParams(vmem_limit_bytes=VMEM),
        name="solve_panel",
    )(panel, rhs, *flat)


def spline_weights(position):
    first = (1.0 - position) ** 3 / 6.0
    second = (3.0 * position**3 - 6.0 * position**2 + 4.0) / 6.0
    third = (-3.0 * position**3 + 3.0 * position**2 + 3.0 * position + 1.0) / 6.0
    fourth = position**3 / 6.0
    return first, second, third, fourth


def gather_kernel(loads, parts, contact_ref, basis_ref, out_ref, wide_basis, weights, gathered):
    step = pl.program_id(0)
    registers = parts // 2
    together = 8 // parts
    row_at = lax.broadcasted_iota(jnp.int32, (8, 128), 0)

    @pl.when(step == 0)
    def _():
        at = lax.broadcasted_iota(jnp.int32, (8 * registers, 128), 0)
        tap = at // parts

        def fill(index, carry):
            position = (index * jnp.ones_like(at)).astype(jnp.float32) / 64.0
            first, second, third, fourth = spline_weights(position)
            value = jnp.where(tap == 0, first, jnp.where(tap == 1, second, jnp.where(tap == 2, third, fourth)))
            weights[pl.ds(pl.multiple_of(index * 8 * registers, 8), 8 * registers), :] = value
            return carry

        lax.fori_loop(0, 64, fill, 0)

    @pl.when(step < loads)
    def _():
        block = basis_ref.shape[0]
        base = step * block

        def widen(index, carry):
            first = pl.multiple_of(index * 16, 16)
            value = basis_ref[pl.ds(first, 16), :].astype(jnp.float32)
            for half in range(2):
                for part in range(parts):
                    at = (base + first + 8 * half) * parts + part
                    wide_basis[pl.ds(at, 8, stride=parts), :] = value[
                        8 * half : 8 * half + 8, 128 * part : 128 * part + 128
                    ]
            return carry

        lax.fori_loop(0, block // 16, widen, 0, unroll=4)

    @pl.when(step >= loads)
    def _():
        block = out_ref.shape[0]
        base = (step - loads) * block

        def pick(index, carry):
            value = None
            for member in range(together):
                contact = contact_ref[base + index * together + member]
                start = (contact >> 6) * parts
                frac = pl.multiple_of((contact & 63) * 8 * registers, 8)
                total = None
                for k in range(registers):
                    term = wide_basis[pl.ds(start + 8 * k, 8), :] * weights[pl.ds(frac + 8 * k, 8), :]
                    total = term if total is None else total + term
                shift = 4
                while shift >= parts:
                    total = total + pltpu.roll(total, shift, 0)
                    shift //= 2
                value = total if value is None else jnp.where(row_at >= member * parts, total, value)
            gathered[pl.ds(pl.multiple_of(index * 8, 8), 8), :] = value
            return carry

        lax.fori_loop(0, block // together, pick, 0, unroll=8)

        def narrow(index, carry):
            first = pl.multiple_of(index * 16, 16)
            pieces = []
            for part in range(parts):
                halves = [
                    gathered[pl.ds((first + 8 * half) * parts + part, 8, stride=parts), :] for half in range(2)
                ]
                pieces.append(jnp.concatenate(halves, axis=0))
            out_ref[pl.ds(first, 16), :] = jnp.concatenate(pieces, axis=1).astype(jnp.bfloat16)
            return carry

        lax.fori_loop(0, block // 16, narrow, 0, unroll=4)


def gather_columns(contact, basis_cols):
    points, columns = basis_cols.shape
    rows = contact.shape[0]
    parts = columns // 128
    in_block, out_block = 1024, 1024
    loads = points // in_block
    return pl.pallas_call(
        functools.partial(gather_kernel, loads, parts),
        grid_spec=pltpu.PrefetchScalarGridSpec(
            num_scalar_prefetch=1,
            grid=(loads + rows // out_block,),
            in_specs=[pl.BlockSpec((in_block, columns), lambda i, c: (jnp.minimum(i, loads - 1), 0))],
            out_specs=pl.BlockSpec((out_block, columns), lambda i, c: (jnp.maximum(i - loads, 0), 0)),
            scratch_shapes=[
                pltpu.VMEM((points * parts, 128), jnp.float32),
                pltpu.VMEM((64 * 4 * parts, 128), jnp.float32),
                pltpu.VMEM((out_block * parts, 128), jnp.float32),
            ],
        ),
        out_shape=jax.ShapeDtypeStruct((rows, columns), jnp.bfloat16),
        compiler_params=pltpu.CompilerParams(vmem_limit_bytes=VMEM),
        name="gather_columns",
    )(contact, basis_cols)


def piece_for(pieces, group, member, distance):
    return lax.dynamic_index_in_dim(pieces, (member + distance) % len(group(0)), 0, keepdims=False)


def shift(piece, axis, group, distance):
    pairs = []
    for device in range(lax.axis_size(axis)):
        members = group(device)
        pairs.append((device, members[(members.index(device) + distance) % len(members)]))
    return lax.ppermute(piece, axis, pairs)


def exchange(pieces, axis, group, member):
    return [
        shift(piece_for(pieces, group, member, distance), axis, group, distance)
        for distance in range(1, len(group(0)))
    ]


def spread(piece, axis, group, member, beside=None):
    size = len(group(0))
    rows = piece.shape[0]
    total = jnp.zeros((size * rows,) + piece.shape[1:], piece.dtype)
    start = (0,) * (piece.ndim - 1)
    total = lax.dynamic_update_slice(total, piece, (member * rows,) + start)
    others = [shift(piece, axis, group, distance) for distance in range(1, size)]
    if beside is not None:
        others, beside = lax.optimization_barrier((others, beside))
    for distance, other in enumerate(others, 1):
        total = lax.dynamic_update_slice(total, other, (((member - distance) % size) * rows,) + start)
    return total if beside is None else (total, beside)


def reduce_to_owner(total, axis, group, member, sent):
    size = len(group(0))
    pieces = total.reshape((size, total.shape[0] // size) + total.shape[1:])
    own = lax.dynamic_index_in_dim(pieces, member, 0, keepdims=False)
    for other in exchange(pieces.astype(sent), axis, group, member):
        own = own + other.astype(jnp.float32)
    return own


def plane_plan(wide_size):
    at = lax.axis_index("wide")
    return [
        ("wide", lambda device: [device & ~1, device | 1], at % 2),
        ("wide", lambda device: list(range(device & 1, wide_size, 2)), at // 2),
    ]


def sum_at_owner(total, plan):
    for step in plan:
        total = reduce_to_owner(total, *step, jnp.bfloat16)
    return total.astype(jnp.bfloat16)


def transposed_product(left, right):
    return lax.dot_general(left, right, (((0,), (0,)), ((), ())), preferred_element_type=jnp.float32)


def per_device(start_point, frac_step, targets, basis_cols):
    wide_size, narrow_size = lax.axis_size("wide"), lax.axis_size("narrow")
    narrow_at = lax.axis_index("narrow")
    rows, width = start_point.shape[0], basis_cols.shape[1]
    order = narrow_size * width
    plane = plane_plan(wide_size)
    line = ("narrow", lambda device: list(range(narrow_size)), narrow_at)

    contact = jnp.stack(
        [start_point.astype(jnp.float32), frac_step.astype(jnp.float32), targets.astype(jnp.float32)]
    )
    contact = lax.all_gather(contact, "narrow", axis=1, tiled=True)
    packed = contact[0].astype(jnp.int32) * 64 + contact[1].astype(jnp.int32)
    group_targets = contact[2].astype(jnp.bfloat16)
    columns = gather_columns(packed, basis_cols)

    pieces = columns.reshape(narrow_size, rows, width)
    outgoing = [piece_for(pieces, line[1], narrow_at, distance) for distance in range(1, narrow_size)]
    received = [shift(outgoing[0], *line[:2], 1)]

    square = transposed_product(columns, columns).reshape(wide_size, width // wide_size, width)
    weighted = lax.dot_general(
        jnp.broadcast_to(group_targets, (8,) + group_targets.shape),
        columns,
        (((1,), (0,)), ((), ())),
        preferred_element_type=jnp.float32,
    )
    square = jnp.concatenate([square, jnp.broadcast_to(weighted, (wide_size, 8, width))], axis=1)
    square = square.reshape(wide_size // 2, 2, -1, width).swapaxes(0, 1).reshape(wide_size, -1, width)
    for step in plane:
        square = reduce_to_owner(square, *step, jnp.float32)
    square, received = lax.optimization_barrier((square, received))
    square = spread(square, *line)
    square, outgoing = lax.optimization_barrier((square, outgoing[1:]))
    received += [shift(piece, *line[:2], distance) for distance, piece in enumerate(outgoing, 2)]
    first_square, later_squares = square[None, :1], square[None, 1:]
    for step in reversed(plane):
        first_square = spread(first_square, *step)
    for step in reversed(plane):
        later_squares = spread(later_squares, *step)
    first_square, later_squares = [
        value.reshape(2, wide_size // 2, *value.shape[1:]).swapaxes(0, 1).reshape(value.shape)
        for value in (first_square, later_squares)
    ]
    inverses = [invert_stage(0, first_square, 0, [])]
    received, inverses = lax.optimization_barrier((received, inverses))

    own = lax.dynamic_index_in_dim(pieces, narrow_at, 0, keepdims=False)
    panel = jnp.zeros((rows, order), jnp.bfloat16)
    panel = lax.dynamic_update_slice(panel, own, (0, narrow_at * width))
    for distance, piece in enumerate(received, 1):
        source = (narrow_at - distance) % narrow_size
        panel = lax.dynamic_update_slice(panel, piece, (0, source * width))

    parts = [
        transposed_product(panel[:, (stage + 1) * width :], panel[:, stage * width : (stage + 1) * width])
        for stage in range(narrow_size - 1)
    ]
    plan = plane + [line]
    off_first = sum_at_owner(parts[0], plan)
    off_later = sum_at_owner(jnp.concatenate(parts[1:], axis=0), plan)
    for step in reversed(plan):
        off_first = spread(off_first, *step)

    below = order - width
    lowers = [below_stage(0, below, off_first, 0, inverses[0], [])]
    inverses.append(invert_stage(1, later_squares, 0, lowers))
    off_later, lowers = spread(off_later, *line, lowers)
    off_later, inverses = spread(off_later, *plane[1], inverses)
    off_later = spread(off_later, *plane[0])
    offset = 0
    for stage in range(1, narrow_size):
        if stage > 1:
            inverses.append(invert_stage(stage, later_squares, stage - 1, lowers))
        below -= width
        if below:
            lowers.append(below_stage(stage, below, off_later, offset, inverses[stage], lowers))
        offset += below
    weighted = jnp.concatenate([first_square[0, :, -8:, :], later_squares[0, :, -8:, :]], axis=0)
    weighted = weighted.transpose(1, 0, 2).reshape(8, order)
    rows_total = rows * wide_size * narrow_size
    q_scaled, coefficients = solve_panel(panel, weighted, inverses, lowers, math.sqrt(rows_total))
    return q_scaled, coefficients.reshape(order)


def solution(mesh):
    rows_at = P(("wide", "narrow"))
    return jax.shard_map(
        per_device,
        mesh=mesh,
        in_specs=(rows_at, rows_at, rows_at, P(None, "narrow")),
        out_specs=(P(("wide", "narrow"), None), P()),
        check_vma=False,
    )
```

time: 726 us -> 403 us (0.56)
  waiting for transfers between devices: 280 us -> 90.2 us
  blocking collectives: 120 us -> 14.9 us
  local copies, waits for them, and re-layouts: 121 us -> 20.8 us
  starting transfers between devices: 0.04 us -> 73.2 us
  Pallas kernels: 162 us -> 180 us
  between operations: 14.5 us -> 1.74 us
    psum x1 -> x0, waiting for transfers between devices: 280 us -> none  [per_device(): summed = lax.psum(gram_local, ('wide', 'narrow'))]
    gather x4 -> x0, local copies, waits for them, and re-layouts: 101 us -> none  [project(): jnp.take(basis_cols, start_point + offset, axis=0).astype(jnp.float32)]
    all_to_all x1 -> x0, blocking collectives: 92.1 us -> none  [per_device(): lax.all_to_all(columns, 'narrow', split_axis=0, concat_axis=1, tiled=True)]
    ppermute x0 -> x46, waiting for transfers between devices: none -> 90.2 us  [shift(): return lax.ppermute(piece, axis, pairs)]
    ppermute x0 -> x46, starting transfers between devices: none -> 73.2 us  [shift(): return lax.ppermute(piece, axis, pairs)]
    slice x6 -> x1, local copies, waits for them, and re-layouts: 16.7 us -> 0.06 us  [per_device(): group_targets = contact[2].astype(jnp.bfloat16)]
    pallas_call x5 -> x8, Pallas kernels: 138 us -> 152 us  [the longest x4 102 us: invert_stage(): pl.pallas_call(functools.partial(invert_kernel, stage), grid=(1,), out_sh...]
    all_gather x2 -> x1, blocking collectives: 28.2 us -> 14.9 us  [per_device(): contact = lax.all_gather(contact, 'narrow', axis=1, tiled=True)]
  transfers between devices with their start and end apart: 1 -> 46, of which waited for: 1 -> 22; matrix products, arithmetic and copies ran while one was open for 0% -> 5% of each run, Pallas kernels for 0% -> 14%
where the time goes in v2:
time: 403 us; the launch traced here: 398 us
  Pallas kernels  180 us (45%)
  waiting for transfers between devices  90.2 us (22%)
  starting transfers between devices  73.2 us (18%)
  local copies, waits for them, and re-layouts  20.8 us (5%)
  blocking collectives  14.9 us (4%)
  matrix products  10.4 us (3%)
  other arithmetic  6.74 us (2%)
    pallas_call x4, Pallas kernels, invert_stage(): pl.pallas_call(functools.partial(invert_kernel, stage), grid=(1,), out_sh...  102 us
    ppermute x46, waiting for transfers between devices, shift(): return lax.ppermute(piece, axis, pairs)  90.2 us
    ppermute x46, starting transfers between devices, shift(): return lax.ppermute(piece, axis, pairs)  73.2 us
    pallas_call x1, Pallas kernels, gather_columns(): pl.pallas_call(functools.partial(gather_kernel, loads, parts), grid_spec=...  28.1 us
    pallas_call x1, Pallas kernels, solve_panel(): pl.pallas_call(functools.partial(q_kernel, count, scale), grid=(rows // t...  27.9 us
    pallas_call x3, Pallas kernels, below_stage(): pl.pallas_call(functools.partial(below_kernel, stage, offset), out_shape=...  22.7 us
    all_gather x1, blocking collectives, per_device(): contact = lax.all_gather(contact, 'narrow', axis=1, tiled=True)  14.9 us
    dot_general x4, matrix products, transposed_product(): lax.dot_general(left, right, (((0,), (0,)), ((), ())), preferred_element_...  9.81 us
  transfers between devices with their start and end apart: 46, of which 22 were waited for; matrix products, arithmetic and copies ran while one was open for 5% of the time, Pallas kernels for 14%

profile of v2, /device:TPU:0, one launch (start us, length us, event | category | flops | bytes accessed | tf_op | source)
XLA Modules:
  0.0 398.4 jit_solution(8083856259336851990)
XLA Ops:
  2.7 14.9 %all_gather.3 = f32[3,4096]{1,0:T(4,128)S(1)} all-gather(f32[3,1024]{1,0:T(4,128)S(1)} %pad_maximum_fusion.2), channel_id=1, replica_groups=mesh['wide'=8,'narrow'=4] {'narrow'}, dimensions={1}, use_global_device_ids=true | all-gather | bytes 61440 | tf_op jit(solution)/shard_map/all_gather | solution.py:409
  18.3 28.1 %gather_columns.1 = bf16[4096,512]{1,0:T(8,128)(2,1)} custom-call(s32[4096]{0:T(1024)} %bitcast.140, bf16[16384,512]{1,0:T(8,128)(2,1)} %basis_ref.1), custom_call_target="tpu_custom_call" | custom-call | tf_op jit(solution)/shard_map/gather_columns/pallas_call | solution.py:319
  46.4 5.9 %fusion.33 = f32[512,512]{1,0:T(8,128)S(1)} fusion(bf16[4096,512]{1,0:T(8,128)(2,1)} %gather_columns.1), kind=kOutput, calls=%fused_computation.112 | convolution fusion | flops 2147483648 | bytes 5242880 | tf_op jit(solution)/shard_map/dot_general | solution.py:395
  53.2 3.5 dynamic-slice_bitcast_fusion
  68.8 15.5 %collective-permute-done.4 = bf16[1024,512]{1,0:T(8,128)(2,1)S(1)} collective-permute-done((bf16[1024,512]{1,0:T(8,128)(2,1)}, bf16[1024,512]{1,0:T(8,128)(2,1)S(1)}, u32[]{:S(2)}, u32[]{:S(2)}) %collective-permute-start.4) | collective-permute-done | bytes 1048608 | tf_op jit(solution)/shard_map/ppermute | solution.py:347
  88.2 4.7 %collective-permute-done.5 = f32[1,72,512]{2,1,0:T(8,128)S(1)} collective-permute-done((f32[1,72,512]{2,1,0:T(8,128)S(1)}, f32[1,72,512]{2,1,0:T(8,128)S(1)}, u32[]{:S(2)}, u32[]{:S(2)}) %collective-permute-start.5) | collective-permute-done | bytes 147488 | tf_op jit(solution)/shard_map/ppermute | solution.py:347
  93.0 5.0 %collective-permute-done.6 = f32[1,72,512]{2,1,0:T(8,128)S(1)} collective-permute-done((f32[1,72,512]{2,1,0:T(8,128)S(1)}, f32[1,72,512]{2,1,0:T(8,128)S(1)}, u32[]{:S(2)}, u32[]{:S(2)}) %collective-permute-start.6) | collective-permute-done | bytes 147488 | tf_op jit(solution)/shard_map/ppermute | solution.py:347
  104.4 3.5 collective-permute-start.9
  111.5 23.2 %invert_diagonal.4 = (bf16[512,512]{1,0:T(8,128)(2,1)}, bf16[512,512]{1,0:T(8,128)(2,1)}) custom-call(f32[8,1,72,512]{3,2,1,0:T(8,128)} %bitcast.126), custom_call_target="tpu_custom_call" | custom-call | flops 1000000 | bytes 1048576 | tf_op jit(solution)/shard_map/invert_diagonal/pallas_call | solution.py:124
  134.6 17.2 %collective-permute-done.8 = bf16[1024,512]{1,0:T(8,128)(2,1)S(1)} collective-permute-done((bf16[1024,512]{1,0:T(8,128)(2,1)}, bf16[1024,512]{1,0:T(8,128)(2,1)S(1)}, u32[]{:S(2)}, u32[]{:S(2)}) %collective-permute-start.8) | collective-permute-done | bytes 1048608 | tf_op jit(solution)/shard_map/ppermute | solution.py:347
  169.8 6.0 %collective-permute-done.14 = f32[1,3,72,512]{3,2,1,0:T(8,128)S(1)} collective-permute-done((f32[1,3,72,512]{3,2,1,0:T(8,128)S(1)}, f32[1,3,72,512]{3,2,1,0:T(8,128)S(1)}, u32[]{:S(2)}, u32[]{:S(2)}) %collective-permute-start.14) | collective-permute-done | bytes 442400 | tf_op jit(solution)/shard_map/ppermute | solution.py:347
  175.9 9.5 %collective-permute-done.15 = f32[1,3,72,512]{3,2,1,0:T(8,128)S(1)} collective-permute-done((f32[1,3,72,512]{3,2,1,0:T(8,128)S(1)}, f32[1,3,72,512]{3,2,1,0:T(8,128)S(1)}, u32[]{:S(2)}, u32[]{:S(2)}) %collective-permute-start.15) | collective-permute-done | bytes 442400 | tf_op jit(solution)/shard_map/ppermute | solution.py:347
  185.4 4.2 %collective-permute-done.29 = bf16[192,512]{1,0:T(8,128)(2,1)S(1)} collective-permute-done((bf16[192,512]{1,0:T(8,128)(2,1)S(1)}, bf16[192,512]{1,0:T(8,128)(2,1)S(1)}, u32[]{:S(2)}, u32[]{:S(2)}) %collective-permute-start.29) | collective-permute-done | bytes 196640 | tf_op jit(solution)/shard_map/ppermute | solution.py:347
  192.6 20.1 %collective-permute-start.32 = (bf16[48,512]{1,0:T(8,128)(2,1)S(1)}, bf16[48,512]{1,0:T(8,128)(2,1)S(1)}, u32[]{:S(2)}, u32[]{:S(2)}) collective-permute-start(bf16[48,512]{1,0:T(8,128)(2,1)S(1)} %get-tuple-element.94), channel_id=1, source_target_pairs={{0,1},{1,2},{2,3},{3,0},{4,5},{5,6},{6,7},{7,4},{8,9},{9,10},{10,1... | collective-permute-start | bytes 147464 | tf_op jit(solution)/shard_map/ppermute | solution.py:347
  212.7 3.3 collective-permute-start.33
  227.3 4.2 %collective-permute-done.36 = bf16[48,512]{1,0:T(8,128)(2,1)S(1)} collective-permute-done((bf16[48,512]{1,0:T(8,128)(2,1)S(1)}, bf16[48,512]{1,0:T(8,128)(2,1)S(1)}, u32[]{:S(2)}, u32[]{:S(2)}) %collective-permute-start.36) | collective-permute-done | bytes 49184 | tf_op jit(solution)/shard_map/ppermute | solution.py:347
  244.5 4.6 %collective-permute-start.23 = (bf16[48,512]{1,0:T(8,128)(2,1)S(1)}, bf16[48,512]{1,0:T(8,128)(2,1)S(1)}, u32[]{:S(2)}, u32[]{:S(2)}) collective-permute-start(bf16[48,512]{1,0:T(8,128)(2,1)S(1)} %get-tuple-element.99), channel_id=1, source_target_pairs={{0,2},{1,3},{2,0},{3,1},{4,6},{5,7},{6,4},{7,5},{8,10},{9,11},{10,... | collective-permute-start | bytes 147464 | tf_op jit(solution)/shard_map/ppermute | solution.py:347
  261.4 7.0 %factor_below.3 = (bf16[1536,512]{1,0:T(8,128)(2,1)}, bf16[1536,512]{1,0:T(8,128)(2,1)}) custom-call(bf16[1536,512]{1,0:T(8,128)(2,1)} %copy-done.6, bf16[512,512]{1,0:T(8,128)(2,1)} %get-tuple-element.59.inv_high.refs_0_, bf16[512,512]{1,0:T(8,128)(2,1)} %get-tuple-element.60.inv_low.refs_1_), custom_call_target="tpu_custom_call" | custom-call | flops 2415919104 | bytes 6291456 | tf_op jit(solution)/shard_map/factor_below/pallas_call | solution.py:162
  272.2 25.0 %invert_diagonal.5 = (bf16[512,512]{1,0:T(8,128)(2,1)}, bf16[512,512]{1,0:T(8,128)(2,1)}) custom-call(f32[8,3,72,512]{3,2,1,0:T(8,128)} %bitcast.129, bf16[1536,512]{1,0:T(8,128)(2,1)} %get-tuple-element.63.refs_0_.refs_8_, bf16[1536,512]{1,0:T(8,128)(2,1)} %get-tuple-element.64.refs_1_.refs_9_), custom_call_target="tpu_custom_call" | custom-call | flops 24999999488 | bytes 1048576 | tf_op jit(solution)/shard_map/invert_diagonal/pallas_call | solution.py:124
  301.1 8.4 %factor_below.4 = (bf16[1024,512]{1,0:T(8,128)(2,1)}, bf16[1024,512]{1,0:T(8,128)(2,1)}) custom-call(bf16[1536,512]{1,0:T(8,128)(2,1)} %copy-done.5, bf16[512,512]{1,0:T(8,128)(2,1)} %get-tuple-element.61.inv_high.refs_2_, bf16[512,512]{1,0:T(8,128)(2,1)} %get-tuple-element.62.inv_low.refs_3_, bf16[1536,512]{1,0:T(8,128)(2,1)} %get-tuple-element.63.refs_0_.refs_8_, ...), custom_call_target="tpu_custom_call" | custom-call | flops 3221225472 | bytes 4194304 | tf_op jit(solution)/shard_map/factor_below/pallas_call | solution.py:162
  309.5 26.1 %invert_diagonal.6 = (bf16[512,512]{1,0:T(8,128)(2,1)}, bf16[512,512]{1,0:T(8,128)(2,1)}) custom-call(f32[8,3,72,512]{3,2,1,0:T(8,128)} %bitcast.131, bf16[1536,512]{1,0:T(8,128)(2,1)} %get-tuple-element.63.refs_0_.refs_8_, bf16[1536,512]{1,0:T(8,128)(2,1)} %get-tuple-element.64.refs_1_.refs_9_, bf16[1024,512]{1,0:T(8,128)(2,1)} %get-tuple-element.68.refs_2_.refs_10_, ...), custom_call_target="tpu_custom_call" | custom-call | flops 24999999488 | bytes 1048576 | tf_op jit(solution)/shard_map/invert_diagonal/pallas_call | solution.py:124
  335.7 7.2 %factor_below.5 = (bf16[512,512]{1,0:T(8,128)(2,1)}, bf16[512,512]{1,0:T(8,128)(2,1)}) custom-call(bf16[1536,512]{1,0:T(8,128)(2,1)} %copy-done.5, bf16[512,512]{1,0:T(8,128)(2,1)} %get-tuple-element.70.inv_high.refs_4_, bf16[512,512]{1,0:T(8,128)(2,1)} %get-tuple-element.71.inv_low.refs_5_, bf16[1536,512]{1,0:T(8,128)(2,1)} %get-tuple-element.63.refs_0_.refs_8_, ...), custom_call_target="tpu_custom_call" | custom-call | flops 2415919104 | bytes 2097152 | tf_op jit(solution)/shard_map/factor_below/pallas_call | solution.py:162
  342.9 27.4 %invert_diagonal.7 = (bf16[512,512]{1,0:T(8,128)(2,1)}, bf16[512,512]{1,0:T(8,128)(2,1)}) custom-call(f32[8,3,72,512]{3,2,1,0:T(8,128)} %bitcast.132, bf16[1536,512]{1,0:T(8,128)(2,1)} %get-tuple-element.63.refs_0_.refs_8_, bf16[1536,512]{1,0:T(8,128)(2,1)} %get-tuple-element.64.refs_1_.refs_9_, bf16[1024,512]{1,0:T(8,128)(2,1)} %get-tuple-element.68.refs_2_.refs_10_, ...), custom_call_target="tpu_custom_call" | custom-call | flops 24999999488 | bytes 1048576 | tf_op jit(solution)/shard_map/invert_diagonal/pallas_call | solution.py:124
  370.3 27.9 %solve_panel.1 = (f32[1024,2048]{1,0:T(8,128)}, f32[1,2048]{1,0:T(1,128)}) custom-call(bf16[1024,2048]{1,0:T(8,128)(2,1)} %copy-done.1, f32[8,2048]{1,0:T(8,128)} %bitcast.139, bf16[512,512]{1,0:T(8,128)(2,1)} %get-tuple-element.59.inv_high.refs_0_, bf16[512,512]{1,0:T(8,128)(2,1)} %get-tuple-element.60.inv_low.refs_1_, ...), custom_call_target="tpu_custom_call" | custom-call | tf_op jit(solution)/shard_map/solve_panel/pallas_call | solution.py:212
  (182 shorter events, 94.1 us)
Async XLA Ops:
  56.8 27.5 %collective-permute-start.4 = (bf16[1024,512]{1,0:T(8,128)(2,1)}, bf16[1024,512]{1,0:T(8,128)(2,1)S(1)}, u32[]{:S(2)}, u32[]{:S(2)}) collective-permute-start(bf16[1024,512]{1,0:T(8,128)(2,1)} %get-tuple-element.84), channel_id=1, source_target_pairs={{0,1},{1,2},{2,3},{3,0},{4,5},{5,6},{6,7},{7,4},{8,9},{9,10},{10,1... | collective-permute-start | bytes 3145736 | tf_op jit(solution)/shard_map/ppermute | solution.py:347
  84.3 13.7 %collective-permute-start.6 = (f32[1,72,512]{2,1,0:T(8,128)S(1)}, f32[1,72,512]{2,1,0:T(8,128)S(1)}, u32[]{:S(2)}, u32[]{:S(2)}) collective-permute-start(f32[1,72,512]{2,1,0:T(8,128)S(1)} %add_add_fusion), channel_id=1, source_target_pairs={{0,2},{1,3},{2,0},{3,1},{4,6},{5,7},{6,4},{7,5},{8,10},{9,11},{10,... | collective-permute-start | bytes 442376 | tf_op jit(solution)/shard_map/ppermute | solution.py:347
  86.6 11.5 %collective-permute-start.7 = (f32[1,72,512]{2,1,0:T(8,128)S(1)}, f32[1,72,512]{2,1,0:T(8,128)S(1)}, u32[]{:S(2)}, u32[]{:S(2)}) collective-permute-start(f32[1,72,512]{2,1,0:T(8,128)S(1)} %add_add_fusion), channel_id=1, source_target_pairs={{0,3},{1,0},{2,1},{3,2},{4,7},{5,4},{6,5},{7,6},{8,11},{9,8},{10,9... | collective-permute-start | bytes 442376 | tf_op jit(solution)/shard_map/ppermute | solution.py:347
  98.1 9.8 %collective-permute-start.10 = (f32[1,1,72,512]{3,2,0,1:T(8,128)S(1)}, f32[1,1,72,512]{3,2,0,1:T(8,128)S(1)}, u32[]{:S(2)}, u32[]{:S(2)}) collective-permute-start(f32[1,1,72,512]{3,2,0,1:T(8,128)S(1)} %slice_bitcast_fusion.1), channel_id=1, source_target_pairs={{0,8},{4,12},{8,16},{12,20},{16,24},{20,28},{24,0},{28,4},{1,9},{5... | collective-permute-start | bytes 442376 | tf_op jit(solution)/shard_map/ppermute | solution.py:347
  102.7 49.2 %collective-permute-start.8 = (bf16[1024,512]{1,0:T(8,128)(2,1)}, bf16[1024,512]{1,0:T(8,128)(2,1)S(1)}, u32[]{:S(2)}, u32[]{:S(2)}) collective-permute-start(bf16[1024,512]{1,0:T(8,128)(2,1)} %get-tuple-element.42), channel_id=1, source_target_pairs={{0,2},{1,3},{2,0},{3,1},{4,6},{5,7},{6,4},{7,5},{8,10},{9,11},{10,... | collective-permute-start | bytes 3145736 | tf_op jit(solution)/shard_map/ppermute | solution.py:347
  104.4 47.5 %collective-permute-start.9 = (bf16[1024,512]{1,0:T(8,128)(2,1)}, bf16[1024,512]{1,0:T(8,128)(2,1)}, u32[]{:S(2)}, u32[]{:S(2)}) collective-permute-start(bf16[1024,512]{1,0:T(8,128)(2,1)} %get-tuple-element.43), channel_id=1, source_target_pairs={{0,3},{1,0},{2,1},{3,2},{4,7},{5,4},{6,5},{7,6},{8,11},{9,8},{10,9... | collective-permute-start | bytes 3145736 | tf_op jit(solution)/shard_map/ppermute | solution.py:347
  161.8 14.0 %collective-permute-start.14 = (f32[1,3,72,512]{3,2,1,0:T(8,128)S(1)}, f32[1,3,72,512]{3,2,1,0:T(8,128)S(1)}, u32[]{:S(2)}, u32[]{:S(2)}) collective-permute-start(f32[1,3,72,512]{3,2,1,0:T(8,128)S(1)} %slice_bitcast_fusion), channel_id=1, source_target_pairs={{0,8},{4,12},{8,16},{12,20},{16,24},{20,28},{24,0},{28,4},{1,9},{5... | collective-permute-start | bytes 1327112 | tf_op jit(solution)/shard_map/ppermute | solution.py:347
  162.4 22.9 %collective-permute-start.15 = (f32[1,3,72,512]{3,2,1,0:T(8,128)S(1)}, f32[1,3,72,512]{3,2,1,0:T(8,128)S(1)}, u32[]{:S(2)}, u32[]{:S(2)}) collective-permute-start(f32[1,3,72,512]{3,2,1,0:T(8,128)S(1)} %slice_bitcast_fusion), channel_id=1, source_target_pairs={{0,16},{4,20},{8,24},{12,28},{16,0},{20,4},{24,8},{28,12},{1,17},{... | collective-permute-start | bytes 1327112 | tf_op jit(solution)/shard_map/ppermute | solution.py:347
  162.9 53.0 %collective-permute-start.16 = (f32[1,3,72,512]{3,2,1,0:T(8,128)S(1)}, f32[1,3,72,512]{3,2,1,0:T(8,128)S(1)}, u32[]{:S(2)}, u32[]{:S(2)}) collective-permute-start(f32[1,3,72,512]{3,2,1,0:T(8,128)S(1)} %slice_bitcast_fusion), channel_id=1, source_target_pairs={{0,24},{4,28},{8,0},{12,4},{16,8},{20,12},{24,16},{28,20},{1,25},{... | collective-permute-start | bytes 1327112 | tf_op jit(solution)/shard_map/ppermute | solution.py:347
  168.1 21.4 %collective-permute-start.29 = (bf16[192,512]{1,0:T(8,128)(2,1)S(1)}, bf16[192,512]{1,0:T(8,128)(2,1)S(1)}, u32[]{:S(2)}, u32[]{:S(2)}) collective-permute-start(bf16[192,512]{1,0:T(8,128)(2,1)S(1)} %get-tuple-element.85), channel_id=1, source_target_pairs={{0,8},{4,12},{8,16},{12,20},{16,24},{20,28},{24,0},{28,4},{1,9},{5... | collective-permute-start | bytes 589832 | tf_op jit(solution)/shard_map/ppermute | solution.py:347
  168.3 24.1 %collective-permute-start.30 = (bf16[192,512]{1,0:T(8,128)(2,1)S(1)}, bf16[192,512]{1,0:T(8,128)(2,1)S(1)}, u32[]{:S(2)}, u32[]{:S(2)}) collective-permute-start(bf16[192,512]{1,0:T(8,128)(2,1)S(1)} %get-tuple-element.87), channel_id=1, source_target_pairs={{0,16},{4,20},{8,24},{12,28},{16,0},{20,4},{24,8},{28,12},{1,17},{... | collective-permute-start | bytes 589832 | tf_op jit(solution)/shard_map/ppermute | solution.py:347
  175.8 16.6 %collective-permute-start.31 = (bf16[192,512]{1,0:T(8,128)(2,1)S(1)}, bf16[192,512]{1,0:T(8,128)(2,1)S(1)}, u32[]{:S(2)}, u32[]{:S(2)}) collective-permute-start(bf16[192,512]{1,0:T(8,128)(2,1)S(1)} %get-tuple-element.86), channel_id=1, source_target_pairs={{0,24},{4,28},{8,0},{12,4},{16,8},{20,12},{24,16},{28,20},{1,25},{... | collective-permute-start | bytes 589832 | tf_op jit(solution)/shard_map/ppermute | solution.py:347
  192.6 25.2 %collective-permute-start.32 = (bf16[48,512]{1,0:T(8,128)(2,1)S(1)}, bf16[48,512]{1,0:T(8,128)(2,1)S(1)}, u32[]{:S(2)}, u32[]{:S(2)}) collective-permute-start(bf16[48,512]{1,0:T(8,128)(2,1)S(1)} %get-tuple-element.94), channel_id=1, source_target_pairs={{0,1},{1,2},{2,3},{3,0},{4,5},{5,6},{6,7},{7,4},{8,9},{9,10},{10,1... | collective-permute-start | bytes 147464 | tf_op jit(solution)/shard_map/ppermute | solution.py:347
  216.0 41.5 %collective-permute-start.17 = (f32[4,3,72,512]{3,2,1,0:T(8,128)S(1)}, f32[4,3,72,512]{3,2,1,0:T(8,128)S(1)}, u32[]{:S(2)}, u32[]{:S(2)}) collective-permute-start(f32[4,3,72,512]{3,2,1,0:T(8,128)S(1)} %constant_dynamic-update-slice_fusion.21), channel_id=1, source_target_pairs={{0,4},{4,0},{8,12},{12,8},{16,20},{20,16},{24,28},{28,24},{1,5},{5... | collective-permute-start | bytes 5308424 | tf_op jit(solution)/shard_map/ppermute | solution.py:347
  220.6 16.4 %collective-permute-start.19 = (bf16[192,512]{1,0:T(8,128)(2,1)S(1)}, bf16[192,512]{1,0:T(8,128)(2,1)S(1)}, u32[]{:S(2)}, u32[]{:S(2)}) collective-permute-start(bf16[192,512]{1,0:T(8,128)(2,1)S(1)} %get-tuple-element.88), channel_id=1, source_target_pairs={{0,8},{4,12},{8,16},{12,20},{16,24},{20,28},{24,0},{28,4},{1,9},{5... | collective-permute-start | bytes 589832 | tf_op jit(solution)/shard_map/ppermute | solution.py:347
  221.7 15.2 %collective-permute-start.20 = (bf16[192,512]{1,0:T(8,128)(2,1)S(1)}, bf16[192,512]{1,0:T(8,128)(2,1)S(1)}, u32[]{:S(2)}, u32[]{:S(2)}) collective-permute-start(bf16[192,512]{1,0:T(8,128)(2,1)S(1)} %get-tuple-element.90), channel_id=1, source_target_pairs={{0,16},{4,20},{8,24},{12,28},{16,0},{20,4},{24,8},{28,12},{1,17},{... | collective-permute-start | bytes 589832 | tf_op jit(solution)/shard_map/ppermute | solution.py:347
  223.3 13.7 %collective-permute-start.21 = (bf16[192,512]{1,0:T(8,128)(2,1)S(1)}, bf16[192,512]{1,0:T(8,128)(2,1)S(1)}, u32[]{:S(2)}, u32[]{:S(2)}) collective-permute-start(bf16[192,512]{1,0:T(8,128)(2,1)S(1)} %get-tuple-element.89), channel_id=1, source_target_pairs={{0,24},{4,28},{8,0},{12,4},{16,8},{20,12},{24,16},{28,20},{1,25},{... | collective-permute-start | bytes 589832 | tf_op jit(solution)/shard_map/ppermute | solution.py:347
  244.3 15.7 %collective-permute-start.41 = (bf16[768,512]{1,0:T(8,128)(2,1)S(1)}, bf16[768,512]{1,0:T(8,128)(2,1)S(1)}, u32[]{:S(2)}, u32[]{:S(2)}) collective-permute-start(bf16[768,512]{1,0:T(8,128)(2,1)S(1)} %constant_dynamic-update-slice_fusion.10), channel_id=1, source_target_pairs={{0,4},{4,0},{8,12},{12,8},{16,20},{20,16},{24,28},{28,24},{1,5},{5... | collective-permute-start | bytes 2359304 | tf_op jit(solution)/shard_map/ppermute | solution.py:347
  253.7 14.7 %collective-permute-start.25 = (bf16[48,512]{1,0:T(8,128)(2,1)S(1)}, bf16[48,512]{1,0:T(8,128)(2,1)S(1)}, u32[]{:S(2)}, u32[]{:S(2)}) collective-permute-start(bf16[48,512]{1,0:T(8,128)(2,1)S(1)} %get-tuple-element.81), channel_id=1, source_target_pairs={{0,1},{1,2},{2,3},{3,0},{4,5},{5,6},{6,7},{7,4},{8,9},{9,10},{10,1... | collective-permute-start | bytes 147464 | tf_op jit(solution)/shard_map/ppermute | solution.py:347
  254.7 13.7 %collective-permute-start.26 = (bf16[48,512]{1,0:T(8,128)(2,1)S(1)}, bf16[48,512]{1,0:T(8,128)(2,1)S(1)}, u32[]{:S(2)}, u32[]{:S(2)}) collective-permute-start(bf16[48,512]{1,0:T(8,128)(2,1)S(1)} %get-tuple-element.81), channel_id=1, source_target_pairs={{0,2},{1,3},{2,0},{3,1},{4,6},{5,7},{6,4},{7,5},{8,10},{9,11},{10,... | collective-permute-start | bytes 147464 | tf_op jit(solution)/shard_map/ppermute | solution.py:347
  256.5 11.9 %collective-permute-start.27 = (bf16[48,512]{1,0:T(8,128)(2,1)S(1)}, bf16[48,512]{1,0:T(8,128)(2,1)S(1)}, u32[]{:S(2)}, u32[]{:S(2)}) collective-permute-start(bf16[48,512]{1,0:T(8,128)(2,1)S(1)} %get-tuple-element.81), channel_id=1, source_target_pairs={{0,3},{1,0},{2,1},{3,2},{4,7},{5,4},{6,5},{7,6},{8,11},{9,8},{10,9... | collective-permute-start | bytes 147464 | tf_op jit(solution)/shard_map/ppermute | solution.py:347
  268.4 28.9 %collective-permute-start.42 = (bf16[192,512]{1,0:T(8,128)(2,1)S(1)}, bf16[192,512]{1,0:T(8,128)(2,1)S(1)}, u32[]{:S(2)}, u32[]{:S(2)}) collective-permute-start(bf16[192,512]{1,0:T(8,128)(2,1)S(1)} %constant_dynamic-update-slice_fusion.5), channel_id=1, source_target_pairs={{0,8},{4,12},{8,16},{12,20},{16,24},{20,28},{24,0},{28,4},{1,9},{5... | collective-permute-start | bytes 589832 | tf_op jit(solution)/shard_map/ppermute | solution.py:347
  270.1 27.3 %collective-permute-start.43 = (bf16[192,512]{1,0:T(8,128)(2,1)S(1)}, bf16[192,512]{1,0:T(8,128)(2,1)S(1)}, u32[]{:S(2)}, u32[]{:S(2)}) collective-permute-start(bf16[192,512]{1,0:T(8,128)(2,1)S(1)} %constant_dynamic-update-slice_fusion.5), channel_id=1, source_target_pairs={{0,16},{4,20},{8,24},{12,28},{16,0},{20,4},{24,8},{28,12},{1,17},{... | collective-permute-start | bytes 589832 | tf_op jit(solution)/shard_map/ppermute | solution.py:347
  271.3 26.0 %collective-permute-start.44 = (bf16[192,512]{1,0:T(8,128)(2,1)S(1)}, bf16[192,512]{1,0:T(8,128)(2,1)S(1)}, u32[]{:S(2)}, u32[]{:S(2)}) collective-permute-start(bf16[192,512]{1,0:T(8,128)(2,1)S(1)} %constant_dynamic-update-slice_fusion.5), channel_id=1, source_target_pairs={{0,24},{4,28},{8,0},{12,4},{16,8},{20,12},{24,16},{28,20},{1,25},{... | collective-permute-start | bytes 589832 | tf_op jit(solution)/shard_map/ppermute | solution.py:347
  (29 other events, 156.0 us)

commit v3 on v2

--- a/solution.py
+++ b/solution.py
@@ -8,7 +8,8 @@
 from jax.experimental.pallas import tpu as pltpu
 from jax.sharding import PartitionSpec as P
 
-VMEM = 56 * 1024 * 1024
+VMEM = 28 * 1024 * 1024
+GATHER_VMEM = 48 * 1024 * 1024
 LEAF = 128
 nt = (((1,), (1,)), ((), ()))
 nn = (((1,), (0,)), ((), ()))
@@ -330,7 +331,7 @@
             ],
         ),
         out_shape=jax.ShapeDtypeStruct((rows, columns), jnp.bfloat16),
-        compiler_params=pltpu.CompilerParams(vmem_limit_bytes=VMEM),
+        compiler_params=pltpu.CompilerParams(vmem_limit_bytes=GATHER_VMEM),
         name="gather_columns",
     )(contact, basis_cols)
 
@@ -454,9 +455,17 @@
         for stage in range(narrow_size - 1)
     ]
     plan = plane + [line]
-    off_first = sum_at_owner(parts[0], plan)
-    off_later = sum_at_owner(jnp.concatenate(parts[1:], axis=0), plan)
-    for step in reversed(plan):
+    off_first = parts[0]
+    off_later = jnp.concatenate(parts[1:], axis=0)
+    for step in plane:
+        off_first = reduce_to_owner(off_first, *step, jnp.bfloat16)
+    off_first, off_later = lax.optimization_barrier((off_first, off_later))
+    off_first = spread(sum_at_owner(off_first, [line]), *line)
+    for step in plane:
+        off_later = reduce_to_owner(off_later, *step, jnp.bfloat16)
+    off_first, off_later = lax.optimization_barrier((off_first, off_later))
+    off_later = sum_at_owner(off_later, [line])
+    for step in reversed(plane):
         off_first = spread(off_first, *step)
 
     below = order - width

time: 403 us -> 364 us (0.903)
  Pallas kernels: 180 us -> 150 us
  waiting for transfers between devices: 90.2 us -> 80.3 us
  starting transfers between devices: 73.2 us -> 82.8 us
    pallas_call x4, Pallas kernels: 102 us -> 88.3 us  [invert_stage(): pl.pallas_call(functools.partial(invert_kernel, stage), grid=(1,), out_sh...]
    pallas_call x3, Pallas kernels: 22.7 us -> 11.1 us  [below_stage(): pl.pallas_call(functools.partial(below_kernel, stage, offset), out_shape=...]
    ppermute x46, waiting for transfers between devices: 90.2 us -> 80.3 us  [shift(): return lax.ppermute(piece, axis, pairs)]
    ppermute x46, starting transfers between devices: 73.2 us -> 82.8 us  [shift(): return lax.ppermute(piece, axis, pairs)]
    pallas_call x1, Pallas kernels: 27.9 us -> 23.6 us  [solve_panel(): pl.pallas_call(functools.partial(q_kernel, count, scale), grid=(rows // t...]
  transfers between devices with their start and end apart: 46 -> 46, of which waited for: 22 -> 20; matrix products, arithmetic and copies ran while one was open for 5% -> 7% of each run, Pallas kernels for 14% -> 13%
where the time goes in v3:
time: 364 us; the launch traced here: 359 us
  Pallas kernels  150 us (41%)
  starting transfers between devices  82.8 us (23%)
  waiting for transfers between devices  80.3 us (22%)
  local copies, waits for them, and re-layouts  19.2 us (5%)
  blocking collectives  14.9 us (4%)
  matrix products  6.87 us (2%)
  other arithmetic  3.7 us (1%)
    pallas_call x4, Pallas kernels, invert_stage(): pl.pallas_call(functools.partial(invert_kernel, stage), grid=(1,), out_sh...  88.3 us
    ppermute x46, starting transfers between devices, shift(): return lax.ppermute(piece, axis, pairs)  82.8 us
    ppermute x46, waiting for transfers between devices, shift(): return lax.ppermute(piece, axis, pairs)  80.3 us
    pallas_call x1, Pallas kernels, gather_columns(): pl.pallas_call(functools.partial(gather_kernel, loads, parts), grid_spec=...  26.6 us
    pallas_call x1, Pallas kernels, solve_panel(): pl.pallas_call(functools.partial(q_kernel, count, scale), grid=(rows // t...  23.6 us
    all_gather x1, blocking collectives, per_device(): contact = lax.all_gather(contact, 'narrow', axis=1, tiled=True)  14.9 us
    pallas_call x3, Pallas kernels, below_stage(): pl.pallas_call(functools.partial(below_kernel, stage, offset), out_shape=...  11.1 us
  transfers between devices with their start and end apart: 46, of which 20 were waited for; matrix products, arithmetic and copies ran while one was open for 7% of the time, Pallas kernels for 13%

profile of v3, /device:TPU:0, one launch (start us, length us, event | category | flops | bytes accessed | tf_op | source)
XLA Modules:
  0.0 359.1 jit_solution(12037072708999478585)
XLA Ops:
  2.7 14.9 %all_gather.3 = f32[3,4096]{1,0:T(4,128)S(1)} all-gather(f32[3,1024]{1,0:T(4,128)S(1)} %pad_maximum_fusion.2), channel_id=1, replica_groups=mesh['wide'=8,'narrow'=4] {'narrow'}, dimensions={1}, use_global_device_ids=true | all-gather | bytes 61440 | tf_op jit(solution)/shard_map/all_gather | solution.py:410
  17.7 26.6 %gather_columns.1 = bf16[4096,512]{1,0:T(8,128)(2,1)S(1)} custom-call(s32[4096]{0:T(1024)S(1)} %bitcast.124, bf16[16384,512]{1,0:T(8,128)(2,1)} %basis_ref.1), custom_call_target="tpu_custom_call" | custom-call | tf_op jit(solution)/shard_map/gather_columns/pallas_call | solution.py:320
  47.6 3.6 dynamic-slice_bitcast_fusion
  57.4 3.2 collective-permute-done.1
  63.1 15.5 %collective-permute-done.4 = bf16[1024,512]{1,0:T(8,128)(2,1)S(1)} collective-permute-done((bf16[1024,512]{1,0:T(8,128)(2,1)}, bf16[1024,512]{1,0:T(8,128)(2,1)S(1)}, u32[]{:S(2)}, u32[]{:S(2)}) %collective-permute-start.4) | collective-permute-done | bytes 1048608 | tf_op jit(solution)/shard_map/ppermute | solution.py:348
  82.6 4.7 %collective-permute-done.5 = f32[1,72,512]{2,1,0:T(8,128)S(1)} collective-permute-done((f32[1,72,512]{2,1,0:T(8,128)S(1)}, f32[1,72,512]{2,1,0:T(8,128)S(1)}, u32[]{:S(2)}, u32[]{:S(2)}) %collective-permute-start.5) | collective-permute-done | bytes 147488 | tf_op jit(solution)/shard_map/ppermute | solution.py:348
  87.3 5.0 %collective-permute-done.6 = f32[1,72,512]{2,1,0:T(8,128)S(1)} collective-permute-done((f32[1,72,512]{2,1,0:T(8,128)S(1)}, f32[1,72,512]{2,1,0:T(8,128)S(1)}, u32[]{:S(2)}, u32[]{:S(2)}) %collective-permute-start.6) | collective-permute-done | bytes 147488 | tf_op jit(solution)/shard_map/ppermute | solution.py:348
  98.7 3.4 collective-permute-start.9
  106.3 20.9 %invert_diagonal.4 = (bf16[512,512]{1,0:T(8,128)(2,1)S(1)}, bf16[512,512]{1,0:T(8,128)(2,1)S(1)}) custom-call(f32[8,1,72,512]{3,2,1,0:T(8,128)S(1)} %bitcast.117), custom_call_target="tpu_custom_call" | custom-call | flops 1000000 | bytes 1048576 | tf_op jit(solution)/shard_map/invert_diagonal/pallas_call | solution.py:125
  127.2 19.1 %collective-permute-done.8 = bf16[1024,512]{1,0:T(8,128)(2,1)} collective-permute-done((bf16[1024,512]{1,0:T(8,128)(2,1)}, bf16[1024,512]{1,0:T(8,128)(2,1)}, u32[]{:S(2)}, u32[]{:S(2)}) %collective-permute-start.8) | collective-permute-done | bytes 1048608 | tf_op jit(solution)/shard_map/ppermute | solution.py:348
  159.9 4.9 %collective-permute-done.19 = bf16[192,512]{1,0:T(8,128)(2,1)S(1)} collective-permute-done((bf16[192,512]{1,0:T(8,128)(2,1)S(1)}, bf16[192,512]{1,0:T(8,128)(2,1)S(1)}, u32[]{:S(2)}, u32[]{:S(2)}) %collective-permute-start.19) | collective-permute-done | bytes 196640 | tf_op jit(solution)/shard_map/ppermute | solution.py:348
  164.8 3.2 collective-permute-done.20
  169.3 20.0 %collective-permute-start.22 = (bf16[48,512]{1,0:T(8,128)(2,1)S(1)}, bf16[48,512]{1,0:T(8,128)(2,1)S(1)}, u32[]{:S(2)}, u32[]{:S(2)}) collective-permute-start(bf16[48,512]{1,0:T(8,128)(2,1)S(1)} %get-tuple-element.105), channel_id=1, source_target_pairs={{0,1},{1,2},{2,3},{3,0},{4,5},{5,6},{6,7},{7,4},{8,9},{9,10},{10,1... | collective-permute-start | bytes 147464 | tf_op jit(solution)/shard_map/ppermute | solution.py:348
  189.2 3.4 collective-permute-start.23
  203.6 10.8 %collective-permute-start.29 = (bf16[192,512]{1,0:T(8,128)(2,1)S(1)}, bf16[192,512]{1,0:T(8,128)(2,1)S(1)}, u32[]{:S(2)}, u32[]{:S(2)}) collective-permute-start(bf16[192,512]{1,0:T(8,128)(2,1)S(1)} %get-tuple-element.93), channel_id=1, source_target_pairs={{0,8},{4,12},{8,16},{12,20},{16,24},{20,28},{24,0},{28,4},{1,9},{5... | collective-permute-start | bytes 589832 | tf_op jit(solution)/shard_map/ppermute | solution.py:348
  217.2 4.0 %collective-permute-done.29 = bf16[192,512]{1,0:T(8,128)(2,1)S(1)} collective-permute-done((bf16[192,512]{1,0:T(8,128)(2,1)S(1)}, bf16[192,512]{1,0:T(8,128)(2,1)S(1)}, u32[]{:S(2)}, u32[]{:S(2)}) %collective-permute-start.29) | collective-permute-done | bytes 196640 | tf_op jit(solution)/shard_map/ppermute | solution.py:348
  227.5 5.1 %collective-permute-done.38 = bf16[192,512]{1,0:T(8,128)(2,1)S(1)} collective-permute-done((bf16[192,512]{1,0:T(8,128)(2,1)S(1)}, bf16[192,512]{1,0:T(8,128)(2,1)S(1)}, u32[]{:S(2)}, u32[]{:S(2)}) %collective-permute-start.38) | collective-permute-done | bytes 196640 | tf_op jit(solution)/shard_map/ppermute | solution.py:348
  249.7 3.7 %factor_below.3 = (bf16[1536,512]{1,0:T(8,128)(2,1)S(1)}, bf16[1536,512]{1,0:T(8,128)(2,1)S(1)}) custom-call(bf16[1536,512]{1,0:T(8,128)(2,1)S(1)} %constant_dynamic-update-slice_fusion.8.off_ref, bf16[512,512]{1,0:T(8,128)(2,1)S(1)} %get-tuple-element.67.inv_high.refs_0_, bf16[512,512]{1,0:T(8,128)(2,1)S(1)} %get-tuple-element.68.inv_low.refs_1_), custom_call_target="tpu_custom_call" | custom-call | flops 2415919104 | bytes 6291456 | tf_op jit(solution)/shard_map/factor_below/pallas_call | solution.py:163
  257.8 21.8 %invert_diagonal.5 = (bf16[512,512]{1,0:T(8,128)(2,1)S(1)}, bf16[512,512]{1,0:T(8,128)(2,1)S(1)}) custom-call(f32[8,3,72,512]{3,2,1,0:T(8,128)S(1)} %bitcast.119, bf16[1536,512]{1,0:T(8,128)(2,1)S(1)} %get-tuple-element.71.refs_0_.refs_8_, bf16[1536,512]{1,0:T(8,128)(2,1)S(1)} %get-tuple-element.72.refs_1_.refs_9_), custom_call_target="tpu_custom_call" | custom-call | flops 24999999488 | bytes 1048576 | tf_op jit(solution)/shard_map/invert_diagonal/pallas_call | solution.py:125
  282.2 4.4 %factor_below.4 = (bf16[1024,512]{1,0:T(8,128)(2,1)S(1)}, bf16[1024,512]{1,0:T(8,128)(2,1)S(1)}) custom-call(bf16[1536,512]{1,0:T(8,128)(2,1)S(1)} %constant_dynamic-update-slice_fusion.38.off_ref, bf16[512,512]{1,0:T(8,128)(2,1)S(1)} %get-tuple-element.69.inv_high.refs_2_, bf16[512,512]{1,0:T(8,128)(2,1)S(1)} %get-tuple-element.70.inv_low.refs_3_, ...), custom_call_target="tpu_custom_call" | custom-call | flops 3221225472 | bytes 4194304 | tf_op jit(solution)/shard_map/factor_below/pallas_call | solution.py:163
  286.6 22.3 %invert_diagonal.6 = (bf16[512,512]{1,0:T(8,128)(2,1)S(1)}, bf16[512,512]{1,0:T(8,128)(2,1)S(1)}) custom-call(f32[8,3,72,512]{3,2,1,0:T(8,128)S(1)} %bitcast.121, bf16[1536,512]{1,0:T(8,128)(2,1)S(1)} %get-tuple-element.71.refs_0_.refs_8_, bf16[1536,512]{1,0:T(8,128)(2,1)S(1)} %get-tuple-element.72.refs_1_.refs_9_, ...), custom_call_target="tpu_custom_call" | custom-call | flops 24999999488 | bytes 1048576 | tf_op jit(solution)/shard_map/invert_diagonal/pallas_call | solution.py:125
  309.0 3.0 factor_below.5
  312.0 23.2 %invert_diagonal.7 = (bf16[512,512]{1,0:T(8,128)(2,1)S(1)}, bf16[512,512]{1,0:T(8,128)(2,1)S(1)}) custom-call(f32[8,3,72,512]{3,2,1,0:T(8,128)S(1)} %bitcast.122, bf16[1536,512]{1,0:T(8,128)(2,1)S(1)} %get-tuple-element.71.refs_0_.refs_8_, bf16[1536,512]{1,0:T(8,128)(2,1)S(1)} %get-tuple-element.72.refs_1_.refs_9_, ...), custom_call_target="tpu_custom_call" | custom-call | flops 24999999488 | bytes 1048576 | tf_op jit(solution)/shard_map/invert_diagonal/pallas_call | solution.py:125
  335.3 23.6 %solve_panel.1 = (f32[1024,2048]{1,0:T(8,128)}, f32[1,2048]{1,0:T(1,128)}) custom-call(bf16[1024,2048]{1,0:T(8,128)(2,1)S(1)} %copy-done.2, f32[8,2048]{1,0:T(8,128)S(1)} %bitcast.123, bf16[512,512]{1,0:T(8,128)(2,1)S(1)} %get-tuple-element.67.inv_high.refs_0_, bf16[512,512]{1,0:T(8,128)(2,1)S(1)} %get-tuple-element.68.inv_low.refs_1_, ...), custom_call_target="tpu_custom_call" | custom-call | tf_op jit(solution)/shard_map/solve_panel/pallas_call | solution.py:213
  (179 shorter events, 86.9 us)
Async XLA Ops:
  51.1 27.5 %collective-permute-start.4 = (bf16[1024,512]{1,0:T(8,128)(2,1)}, bf16[1024,512]{1,0:T(8,128)(2,1)S(1)}, u32[]{:S(2)}, u32[]{:S(2)}) collective-permute-start(bf16[1024,512]{1,0:T(8,128)(2,1)} %get-tuple-element.92), channel_id=1, source_target_pairs={{0,1},{1,2},{2,3},{3,0},{4,5},{5,6},{6,7},{7,4},{8,9},{9,10},{10,1... | collective-permute-start | bytes 3145736 | tf_op jit(solution)/shard_map/ppermute | solution.py:348
  78.7 13.7 %collective-permute-start.6 = (f32[1,72,512]{2,1,0:T(8,128)S(1)}, f32[1,72,512]{2,1,0:T(8,128)S(1)}, u32[]{:S(2)}, u32[]{:S(2)}) collective-permute-start(f32[1,72,512]{2,1,0:T(8,128)S(1)} %add_add_fusion), channel_id=1, source_target_pairs={{0,2},{1,3},{2,0},{3,1},{4,6},{5,7},{6,4},{7,5},{8,10},{9,11},{10,... | collective-permute-start | bytes 442376 | tf_op jit(solution)/shard_map/ppermute | solution.py:348
  80.9 11.5 %collective-permute-start.7 = (f32[1,72,512]{2,1,0:T(8,128)S(1)}, f32[1,72,512]{2,1,0:T(8,128)S(1)}, u32[]{:S(2)}, u32[]{:S(2)}) collective-permute-start(f32[1,72,512]{2,1,0:T(8,128)S(1)} %add_add_fusion), channel_id=1, source_target_pairs={{0,3},{1,0},{2,1},{3,2},{4,7},{5,4},{6,5},{7,6},{8,11},{9,8},{10,9... | collective-permute-start | bytes 442376 | tf_op jit(solution)/shard_map/ppermute | solution.py:348
  92.4 9.7 %collective-permute-start.10 = (f32[1,1,72,512]{3,2,0,1:T(8,128)S(1)}, f32[1,1,72,512]{3,2,0,1:T(8,128)S(1)}, u32[]{:S(2)}, u32[]{:S(2)}) collective-permute-start(f32[1,1,72,512]{3,2,0,1:T(8,128)S(1)} %slice_bitcast_fusion.1), channel_id=1, source_target_pairs={{0,8},{4,12},{8,16},{12,20},{16,24},{20,28},{24,0},{28,4},{1,9},{5... | collective-permute-start | bytes 442376 | tf_op jit(solution)/shard_map/ppermute | solution.py:348
  97.0 49.3 %collective-permute-start.8 = (bf16[1024,512]{1,0:T(8,128)(2,1)}, bf16[1024,512]{1,0:T(8,128)(2,1)}, u32[]{:S(2)}, u32[]{:S(2)}) collective-permute-start(bf16[1024,512]{1,0:T(8,128)(2,1)} %get-tuple-element.46), channel_id=1, source_target_pairs={{0,2},{1,3},{2,0},{3,1},{4,6},{5,7},{6,4},{7,5},{8,10},{9,11},{10,... | collective-permute-start | bytes 3145736 | tf_op jit(solution)/shard_map/ppermute | solution.py:348
  98.7 47.6 %collective-permute-start.9 = (bf16[1024,512]{1,0:T(8,128)(2,1)}, bf16[1024,512]{1,0:T(8,128)(2,1)}, u32[]{:S(2)}, u32[]{:S(2)}) collective-permute-start(bf16[1024,512]{1,0:T(8,128)(2,1)} %get-tuple-element.47), channel_id=1, source_target_pairs={{0,3},{1,0},{2,1},{3,2},{4,7},{5,4},{6,5},{7,6},{8,11},{9,8},{10,9... | collective-permute-start | bytes 3145736 | tf_op jit(solution)/shard_map/ppermute | solution.py:348
  104.3 64.1 %collective-permute-start.14 = (f32[1,3,72,512]{3,2,1,0:T(8,128)S(1)}, f32[1,3,72,512]{3,2,1,0:T(8,128)S(1)}, u32[]{:S(2)}, u32[]{:S(2)}) collective-permute-start(f32[1,3,72,512]{3,2,1,0:T(8,128)S(1)} %slice_bitcast_fusion), channel_id=1, source_target_pairs={{0,8},{4,12},{8,16},{12,20},{16,24},{20,28},{24,0},{28,4},{1,9},{5... | collective-permute-start | bytes 1327112 | tf_op jit(solution)/shard_map/ppermute | solution.py:348
  105.1 87.5 %collective-permute-start.15 = (f32[1,3,72,512]{3,2,1,0:T(8,128)S(1)}, f32[1,3,72,512]{3,2,1,0:T(8,128)S(1)}, u32[]{:S(2)}, u32[]{:S(2)}) collective-permute-start(f32[1,3,72,512]{3,2,1,0:T(8,128)S(1)} %slice_bitcast_fusion), channel_id=1, source_target_pairs={{0,16},{4,20},{8,24},{12,28},{16,0},{20,4},{24,8},{28,12},{1,17},{... | collective-permute-start | bytes 1327112 | tf_op jit(solution)/shard_map/ppermute | solution.py:348
  156.7 11.2 %collective-permute-start.20 = (bf16[192,512]{1,0:T(8,128)(2,1)S(1)}, bf16[192,512]{1,0:T(8,128)(2,1)S(1)}, u32[]{:S(2)}, u32[]{:S(2)}) collective-permute-start(bf16[192,512]{1,0:T(8,128)(2,1)S(1)} %get-tuple-element.98), channel_id=1, source_target_pairs={{0,16},{4,20},{8,24},{12,28},{16,0},{20,4},{24,8},{28,12},{1,17},{... | collective-permute-start | bytes 589832 | tf_op jit(solution)/shard_map/ppermute | solution.py:348
  157.3 10.8 %collective-permute-start.21 = (bf16[192,512]{1,0:T(8,128)(2,1)S(1)}, bf16[192,512]{1,0:T(8,128)(2,1)S(1)}, u32[]{:S(2)}, u32[]{:S(2)}) collective-permute-start(bf16[192,512]{1,0:T(8,128)(2,1)S(1)} %get-tuple-element.97), channel_id=1, source_target_pairs={{0,24},{4,28},{8,0},{12,4},{16,8},{20,12},{24,16},{28,20},{1,25},{... | collective-permute-start | bytes 589832 | tf_op jit(solution)/shard_map/ppermute | solution.py:348
  164.8 33.5 %collective-permute-start.16 = (f32[1,3,72,512]{3,2,1,0:T(8,128)S(1)}, f32[1,3,72,512]{3,2,1,0:T(8,128)S(1)}, u32[]{:S(2)}, u32[]{:S(2)}) collective-permute-start(f32[1,3,72,512]{3,2,1,0:T(8,128)S(1)} %slice_bitcast_fusion), channel_id=1, source_target_pairs={{0,24},{4,28},{8,0},{12,4},{16,8},{20,12},{24,16},{28,20},{1,25},{... | collective-permute-start | bytes 1327112 | tf_op jit(solution)/shard_map/ppermute | solution.py:348
  168.3 34.9 %collective-permute-start.28 = (bf16[768,512]{1,0:T(8,128)(2,1)S(1)}, bf16[768,512]{1,0:T(8,128)(2,1)S(1)}, u32[]{:S(2)}, u32[]{:S(2)}) collective-permute-start(bf16[768,512]{1,0:T(8,128)(2,1)S(1)} %fusion.10), channel_id=1, source_target_pairs={{0,4},{4,0},{8,12},{12,8},{16,20},{20,16},{24,28},{28,24},{1,5},{5... | collective-permute-start | bytes 2359304 | tf_op jit(solution)/shard_map/ppermute | solution.py:348
  169.3 25.5 %collective-permute-start.22 = (bf16[48,512]{1,0:T(8,128)(2,1)S(1)}, bf16[48,512]{1,0:T(8,128)(2,1)S(1)}, u32[]{:S(2)}, u32[]{:S(2)}) collective-permute-start(bf16[48,512]{1,0:T(8,128)(2,1)S(1)} %get-tuple-element.105), channel_id=1, source_target_pairs={{0,1},{1,2},{2,3},{3,0},{4,5},{5,6},{6,7},{7,4},{8,9},{9,10},{10,1... | collective-permute-start | bytes 147464 | tf_op jit(solution)/shard_map/ppermute | solution.py:348
  199.1 43.4 %collective-permute-start.17 = (f32[4,3,72,512]{3,2,1,0:T(8,128)}, f32[4,3,72,512]{3,2,1,0:T(8,128)}, u32[]{:S(2)}, u32[]{:S(2)}) collective-permute-start(f32[4,3,72,512]{3,2,1,0:T(8,128)} %constant_dynamic-update-slice_fusion.21), channel_id=1, source_target_pairs={{0,4},{4,0},{8,12},{12,8},{16,20},{20,16},{24,28},{28,24},{1,5},{5... | collective-permute-start | bytes 5308424 | tf_op jit(solution)/shard_map/ppermute | solution.py:348
  199.1 16.9 %collective-permute-start.26 = (bf16[48,512]{1,0:T(8,128)(2,1)S(1)}, bf16[48,512]{1,0:T(8,128)(2,1)S(1)}, u32[]{:S(2)}, u32[]{:S(2)}) collective-permute-start(bf16[48,512]{1,0:T(8,128)(2,1)S(1)} %get-tuple-element.89), channel_id=1, source_target_pairs={{0,2},{1,3},{2,0},{3,1},{4,6},{5,7},{6,4},{7,5},{8,10},{9,11},{10,... | collective-permute-start | bytes 147464 | tf_op jit(solution)/shard_map/ppermute | solution.py:348
  200.8 16.3 %collective-permute-start.27 = (bf16[48,512]{1,0:T(8,128)(2,1)S(1)}, bf16[48,512]{1,0:T(8,128)(2,1)S(1)}, u32[]{:S(2)}, u32[]{:S(2)}) collective-permute-start(bf16[48,512]{1,0:T(8,128)(2,1)S(1)} %get-tuple-element.89), channel_id=1, source_target_pairs={{0,3},{1,0},{2,1},{3,2},{4,7},{5,4},{6,5},{7,6},{8,11},{9,8},{10,9... | collective-permute-start | bytes 147464 | tf_op jit(solution)/shard_map/ppermute | solution.py:348
  203.6 17.6 %collective-permute-start.29 = (bf16[192,512]{1,0:T(8,128)(2,1)S(1)}, bf16[192,512]{1,0:T(8,128)(2,1)S(1)}, u32[]{:S(2)}, u32[]{:S(2)}) collective-permute-start(bf16[192,512]{1,0:T(8,128)(2,1)S(1)} %get-tuple-element.93), channel_id=1, source_target_pairs={{0,8},{4,12},{8,16},{12,20},{16,24},{20,28},{24,0},{28,4},{1,9},{5... | collective-permute-start | bytes 589832 | tf_op jit(solution)/shard_map/ppermute | solution.py:348
  214.5 9.2 %collective-permute-start.30 = (bf16[192,512]{1,0:T(8,128)(2,1)S(1)}, bf16[192,512]{1,0:T(8,128)(2,1)S(1)}, u32[]{:S(2)}, u32[]{:S(2)}) collective-permute-start(bf16[192,512]{1,0:T(8,128)(2,1)S(1)} %get-tuple-element.95), channel_id=1, source_target_pairs={{0,16},{4,20},{8,24},{12,28},{16,0},{20,4},{24,8},{28,12},{1,17},{... | collective-permute-start | bytes 589832 | tf_op jit(solution)/shard_map/ppermute | solution.py:348
  225.6 9.4 %collective-permute-start.39 = (bf16[192,512]{1,0:T(8,128)(2,1)S(1)}, bf16[192,512]{1,0:T(8,128)(2,1)S(1)}, u32[]{:S(2)}, u32[]{:S(2)}) collective-permute-start(bf16[192,512]{1,0:T(8,128)(2,1)S(1)} %constant_dynamic-update-slice_fusion.15), channel_id=1, source_target_pairs={{0,16},{4,20},{8,24},{12,28},{16,0},{20,4},{24,8},{28,12},{1,17},{... | collective-permute-start | bytes 589832 | tf_op jit(solution)/shard_map/ppermute | solution.py:348
  226.2 8.8 %collective-permute-start.40 = (bf16[192,512]{1,0:T(8,128)(2,1)S(1)}, bf16[192,512]{1,0:T(8,128)(2,1)S(1)}, u32[]{:S(2)}, u32[]{:S(2)}) collective-permute-start(bf16[192,512]{1,0:T(8,128)(2,1)S(1)} %constant_dynamic-update-slice_fusion.15), channel_id=1, source_target_pairs={{0,24},{4,28},{8,0},{12,4},{16,8},{20,12},{24,16},{28,20},{1,25},{... | collective-permute-start | bytes 589832 | tf_op jit(solution)/shard_map/ppermute | solution.py:348
  235.1 14.6 %collective-permute-start.41 = (bf16[768,512]{1,0:T(8,128)(2,1)S(1)}, bf16[768,512]{1,0:T(8,128)(2,1)S(1)}, u32[]{:S(2)}, u32[]{:S(2)}) collective-permute-start(bf16[768,512]{1,0:T(8,128)(2,1)S(1)} %constant_dynamic-update-slice_fusion.10), channel_id=1, source_target_pairs={{0,4},{4,0},{8,12},{12,8},{16,20},{20,16},{24,28},{28,24},{1,5},{5... | collective-permute-start | bytes 2359304 | tf_op jit(solution)/shard_map/ppermute | solution.py:348
  253.5 26.2 %collective-permute-start.42 = (bf16[192,512]{1,0:T(8,128)(2,1)S(1)}, bf16[192,512]{1,0:T(8,128)(2,1)S(1)}, u32[]{:S(2)}, u32[]{:S(2)}) collective-permute-start(bf16[192,512]{1,0:T(8,128)(2,1)S(1)} %constant_dynamic-update-slice_fusion.5), channel_id=1, source_target_pairs={{0,8},{4,12},{8,16},{12,20},{16,24},{20,28},{24,0},{28,4},{1,9},{5... | collective-permute-start | bytes 589832 | tf_op jit(solution)/shard_map/ppermute | solution.py:348
  254.8 24.9 %collective-permute-start.43 = (bf16[192,512]{1,0:T(8,128)(2,1)S(1)}, bf16[192,512]{1,0:T(8,128)(2,1)S(1)}, u32[]{:S(2)}, u32[]{:S(2)}) collective-permute-start(bf16[192,512]{1,0:T(8,128)(2,1)S(1)} %constant_dynamic-update-slice_fusion.5), channel_id=1, source_target_pairs={{0,16},{4,20},{8,24},{12,28},{16,0},{20,4},{24,8},{28,12},{1,17},{... | collective-permute-start | bytes 589832 | tf_op jit(solution)/shard_map/ppermute | solution.py:348
  256.5 23.3 %collective-permute-start.44 = (bf16[192,512]{1,0:T(8,128)(2,1)S(1)}, bf16[192,512]{1,0:T(8,128)(2,1)S(1)}, u32[]{:S(2)}, u32[]{:S(2)}) collective-permute-start(bf16[192,512]{1,0:T(8,128)(2,1)S(1)} %constant_dynamic-update-slice_fusion.5), channel_id=1, source_target_pairs={{0,24},{4,28},{8,0},{12,4},{16,8},{20,12},{24,16},{28,20},{1,25},{... | collective-permute-start | bytes 589832 | tf_op jit(solution)/shard_map/ppermute | solution.py:348
  (27 other events, 217.3 us)
